TPU v7x, 256 devices: a whole 4x4x8 slice. The times are simulated.
256 devices in a mesh: shot: 64 (over z, y, x_hi), slab: 4 (over x_lo, core).
Axes of the slice: x: 4 (x_hi: 2, x_lo: 2; x = x_hi * 2 + x_lo), y: 4, z: 8, core: 2. Of those that a mesh axis runs over, the one named last changes fastest.
Arguments:
- amplitudes: float32 [4, 6144], P('slab', 'shot'), may hold values from -6 to 6
- depth_cells: int32 [4, 6144], P('slab', 'shot'), may hold values from 0 to 63
- lateral_cells: int32 [2, 4, 6144], P(None, 'slab', 'shot'), may hold values from 0 to 511
- jitter: float32 [3, 4, 6144], P(None, 'slab', 'shot'), may hold values from 0 to 1
- tables: float32 [256, 4, 867], P('shot', 'slab'), may hold values from 2 to 509
- shot_cells: int32 [2, 256], P(None, 'shot'), may hold values from 0 to 511
- receiver_offsets: int32 [2, 256], replicated, may hold values from -64 to 63
- band_offsets: int32 [4], replicated, may hold values from 0 to 255
Outputs:
- synthetic: float32 [256, 256, 1024], P('shot')
- image: float32 [4, 6144], P('slab', 'shot')
Inputs may be any that keep to these rules, and one draw needn't show every extreme that they name: Each slab's band lies inside the trace: band_offsets + 512 <= 1024.
All inputs are finite; a program needn't handle non-finite values.
Results may differ from a plain program's by a relative error of at most 0.009.
Values may be sent and summed in bfloat16 or wider, within the bound.
No kernel may reach another device: no remote copies, remote signals or barrier semaphores. Data moves between devices by JAX's collectives and lax.ppermute only.
A program may use at most 64 MiB of HBM per device.

v0:
```python
import math

import jax
import jax.numpy as jnp
from jax import lax
from jax.sharding import PartitionSpec as P

NX = 512
NT = 1024
BAND = 512
SPACING = 32
NL = 17
ND = 3


def node_weights(coords):
    depth_nodes = jnp.arange(ND, dtype=jnp.float32)[:, None]
    lateral_nodes = jnp.arange(NL, dtype=jnp.float32)[:, None]
    weight_z = jnp.maximum(0.0, 1.0 - jnp.abs(coords[0][None, :] / SPACING - depth_nodes))
    weight_x = jnp.maximum(0.0, 1.0 - jnp.abs(coords[1][None, :] / SPACING - lateral_nodes))
    weight_y = jnp.maximum(0.0, 1.0 - jnp.abs(coords[2][None, :] / SPACING - lateral_nodes))
    joined = weight_z[:, None, None, :] * weight_x[None, :, None, :] * weight_y[None, None, :, :]
    return joined.reshape(ND * NL * NL, coords.shape[1])


def block_fields(coords, table, shot_xy, receivers):
    travel = jnp.dot(
        table,
        node_weights(coords),
        precision=lax.Precision.HIGHEST,
        preferred_element_type=jnp.float32,
    )
    samples = jnp.arange(BAND, dtype=jnp.float32)
    hats = jnp.maximum(0.0, 1.0 - jnp.abs(samples[None, None, :] - travel[:, :, None])).astype(
        jnp.bfloat16
    )
    recv_x = shot_xy[0][:, None] + receivers[0][None, :]
    recv_y = shot_xy[1][:, None] + receivers[1][None, :]
    delta_x = recv_x[:, :, None] - coords[1][None, None, :]
    delta_y = recv_y[:, :, None] - coords[2][None, None, :]
    aperture = NX / 32.0
    gain = 1.0 / (1.0 + (delta_x * delta_x + delta_y * delta_y) / (aperture * aperture))
    return (hats, gain)


def body(
    amplitudes,
    depth_cells,
    lateral_cells,
    jitter,
    tables,
    shot_cells,
    receiver_offsets,
    band_offsets,
):
    owned_count = amplitudes.shape[1]
    shots = tables.shape[0]
    receiver_count = receiver_offsets.shape[1]
    shot_xy = shot_cells.astype(jnp.float32)
    receivers = receiver_offsets.astype(jnp.float32)
    table = tables[:, 0, :]
    local_coords = jnp.stack(
        [
            depth_cells[0].astype(jnp.float32) + jitter[0, 0],
            lateral_cells[0, 0].astype(jnp.float32) + jitter[1, 0],
            lateral_cells[1, 0].astype(jnp.float32) + jitter[2, 0],
            amplitudes[0],
        ]
    )
    points = lax.all_gather(local_coords, "shot", axis=1, tiled=True)
    total_count = points.shape[1]
    block = math.gcd(total_count, 1024)

    def demig_step(index, total):
        piece = lax.dynamic_slice_in_dim(points, index * block, block, 1)
        hats, gain = block_fields(piece, table, shot_xy, receivers)
        weighted = (gain * piece[3][None, None, :]).astype(jnp.bfloat16)
        return total + jnp.einsum(
            "srp,spt->srt", weighted, hats, preferred_element_type=jnp.float32
        )

    start = jnp.zeros((shots, receiver_count, BAND), jnp.float32)
    partial_value = lax.fori_loop(0, total_count // block, demig_step, start).astype(jnp.bfloat16)
    slab_index = lax.axis_index("slab")
    my_offset = lax.dynamic_index_in_dim(band_offsets, slab_index, 0, keepdims=False)
    zero = jnp.zeros((), jnp.int32)
    placed = jnp.zeros((shots, receiver_count, NT), jnp.float32)
    placed = lax.dynamic_update_slice(
        placed, partial_value.astype(jnp.float32), (zero, zero, my_offset)
    )
    trace = lax.psum(placed.astype(jnp.bfloat16), "slab").astype(jnp.float32)
    band = lax.dynamic_slice(trace, (zero, zero, my_offset), (shots, receiver_count, BAND)).astype(
        jnp.bfloat16
    )
    step = math.gcd(total_count, 1024)

    def mig_block(index):
        piece = lax.dynamic_slice_in_dim(points, 0 + index * step, step, 1)
        hats, gain = block_fields(piece, table, shot_xy, receivers)
        product = jnp.einsum(
            "srp,srt->spt", gain.astype(jnp.bfloat16), band, preferred_element_type=jnp.float32
        )
        return jnp.sum(product * hats, axis=(0, 2))

    values = lax.map(mig_block, jnp.arange(total_count // step, dtype=jnp.int32))
    summed = lax.psum(values.reshape(total_count) / receiver_count, "shot")
    mine = lax.dynamic_slice_in_dim(summed, lax.axis_index("shot") * owned_count, owned_count, 0)
    return (trace, mine.reshape(1, owned_count))


def solution(mesh):
    placed = (
        P("slab", "shot"),
        P("slab", "shot"),
        P(None, "slab", "shot"),
        P(None, "slab", "shot"),
        P("shot", "slab", None),
        P(None, "shot"),
        P(),
        P(),
    )
    return jax.shard_map(
        body,
        mesh=mesh,
        in_specs=placed,
        out_specs=(P("shot", None, None), P("slab", "shot")),
        check_vma=False,
    )
```

profile of v0, /device:TPU:2, one launch (start us, length us, event | category | flops | bytes accessed | tf_op | source)
XLA Modules:
  0.0 835.0 jit_solution(758956851033260821)
XLA Ops:
  11.9 184.4 %all-gather = f32[64,96,4]{1,2,0:T(4,128)S(1)} all-gather(f32[1,96,4]{1,2,0:T(4,128)S(1)} %maximum_bitcast_fusion), channel_id=1, replica_groups=mesh['shot'=64,'slab'=4] {'shot'}, dimensions={0}, use_global_device_ids=true | all-gather | bytes 99840 | tf_op jit(solution)/shard_map/all_gather | solution.py:70
  198.6 93.8 %while.25 = (s32[]{:T(128)}, f32[4,256,512]{2,1,0:T(8,128)S(1)}, f32[2,4]{1,0:T(2,128)S(1)}, f32[2,256]{1,0:T(2,128)S(1)}, f32[4,6144]{1,0:T(4,128)S(1)}, /*inde...) while((s32[]{:T(128)}, f32[4,256,512]{2,1,0:T(8,128)S(1)}, ...), condition=%wide.region_1.0_spmd.clone, body=%wide.region_0.0_spmd.clone.sunk | while | flops 1139473408 | bytes 19255160 | solution.py:83
  201.6 5.1 mul.263
  206.7 4.2 convolution_bitcast_fusion.5
  217.3 5.1 mul.263
  222.3 4.2 convolution_bitcast_fusion.5
  232.9 5.1 mul.263
  238.0 4.2 convolution_bitcast_fusion.5
  248.5 5.1 mul.263
  253.6 4.2 convolution_bitcast_fusion.5
  264.2 5.1 mul.263
  269.2 4.2 convolution_bitcast_fusion.5
  279.8 5.1 mul.263
  284.9 4.2 convolution_bitcast_fusion.5
  293.4 10.1 %dynamic_update_slice.7 = bf16[4,256,1024]{2,1,0:T(8,128)(2,1)S(1)} dynamic-update-slice(bf16[4,256,1024]{2,1,0:T(8,128)(2,1)S(1)} %broadcast_in_dim.49, bf16[4,256,512]{2,1,0:T(8,128)(2,1)S(1)} %convert_element_type.102, s32[]{:T(128)} %constant.116.clone.1, s32[]{:T(128)} %constant.116.clone.1, s32[]{:T(128)S(6)} %select_n.22) | dynamic-update-slice | bytes 2097156 | tf_op jit(solution)/shard_map/dynamic_update_slice | solution.py:88
  304.9 56.8 %all-reduce.2.cloned.1.call-done = bf16[4,256,1024]{2,1,0:T(8,128)(2,1)} async-done(((bf16[4,256,1024]{2,1,0:T(8,128)(2,1)}), bf16[4,256,1024]{2,1,0:T(8,128)(2,1)}) %all-reduce.2.cloned.1.call-update) | async-done | bytes 2097168 | tf_op jit(solution)/shard_map/psum | solution.py:91
  366.6 102.2 %while.24 = (s32[]{:T(128)}, f32[6,1024]{1,0:T(8,128)S(1)}, f32[2,4]{1,0:T(2,128)S(1)}, f32[2,256]{1,0:T(2,128)S(1)}, s32[6]{0:T(128)S(1)}, /*index=5*/f32[4,614...) while((s32[]{:T(128)}, f32[6,1024]{1,0:T(8,128)S(1)}, ...), condition=%wide.region_5.6_spmd, body=%wide.region_3.5_spmd.sunk | while | flops 1143666688 | bytes 16109431 | solution.py:105
  371.1 5.1 mul.251
  376.2 4.2 convolution_bitcast_fusion.4
  388.1 5.1 mul.251
  393.2 4.2 convolution_bitcast_fusion.4
  405.1 5.1 mul.251
  410.2 4.2 convolution_bitcast_fusion.4
  414.5 3.2 multiply_reduce_fusion.2
  422.1 5.1 mul.251
  427.2 4.2 convolution_bitcast_fusion.4
  439.1 5.1 mul.251
  444.2 4.2 convolution_bitcast_fusion.4
  456.1 5.1 mul.251
  461.3 4.2 convolution_bitcast_fusion.4
  465.5 3.2 multiply_reduce_fusion.2
  468.9 358.7 %psum.15 = f32[6144]{0:T(1024)S(1)} all-reduce(f32[6144]{0:T(1024)S(1)} %div.56), channel_id=1, replica_groups=mesh['shot'=64,'slab'=4] {'shot'}, use_global_device_ids=true, to_apply=%region_6.7 | all-reduce | flops 6144 | bytes 49152 | tf_op jit(solution)/shard_map/psum | solution.py:106
  (156 shorter events, 86.3 us)
Async XLA Ops:
  7.2 354.5 %all-reduce.2.cloned.1.call-start = ((), (), s32[]{:S(2)}) async-start(), calls=%async_computation | async-start | bytes 4194304 | tf_op jit(solution)/shard_map/psum | solution.py:91
  303.5 1.3 copy-start
  363.7 2.0 copy-start.1
Sparse Core Ops, SparseCore 0:
  305.0 56.6 all-reduce.1
where the time goes:
time: 836 us; the launch traced here: 835 us
  blocking collectives  543 us (65%)
  matrix products  88.7 us (11%)
  local copies, waits for them, and re-layouts  82.8 us (10%)
  waiting for transfers between devices  56.8 us (7%)
  other arithmetic  43 us (5%)
  between operations  16.2 us (2%)
    psum x1, blocking collectives, body(): summed = lax.psum(values.reshape(total_count) / receiver_count, 'shot')  359 us
    all_gather x1, blocking collectives, body(): points = lax.all_gather(local_coords, 'shot', axis=1, tiled=True)  184 us
    mul x12, local copies, waits for them, and re-layouts, node_weights(): weight_z[:, None, None, :] * weight_x[None, :, None, :]  61.2 us
    psum x1, waiting for transfers between devices, body(): trace = lax.psum(placed.astype(jnp.bfloat16), 'slab').astype(jnp.float32)  56.8 us
    dot_general x12, matrix products, block_fields(): jnp.dot(table, node_weights(coords), precision=lax.Precision.HIGHEST, pre...  50.6 us
    mul x24, other arithmetic, node_weights(): weight_z[:, None, None, :] * weight_x[None, :, None, :]  34.7 us
    dot_general x6, matrix products, mig_block(): jnp.einsum('srp,srt->spt', gain.astype(jnp.bfloat16), band, preferred_ele...  19.2 us
    dot_general x6, matrix products, demig_step(): jnp.einsum('srp,spt->srt', weighted, hats, preferred_element_type=jnp.flo...  19 us
  transfers between devices with their start and end apart: 1, of which 1 were waited for; matrix products, arithmetic and copies ran while one was open for 0% of the time, Pallas kernels for 0%

commit v1 on v0

v1 whole, which is shorter than its diff:
```python
import functools

import jax
import jax.numpy as jnp
from jax import lax
from jax.experimental import pallas as pl
from jax.experimental.pallas import tpu as pltpu
from jax.sharding import PartitionSpec as P

NX = 512
NT = 1024
BAND = 512
HALF = 256
SPACING = 32
NL = 17
ND = 3
SPAN = 768
LANES = 128
NODE_ROWS = 24
NODE_COLS = 32
ROWS = 8
CHUNK = ROWS * LANES
BF = jnp.bfloat16
F32 = jnp.float32


def split3(value):
    first = value.astype(BF)
    rest = value - first.astype(F32)
    second = rest.astype(BF)
    third = (rest - second.astype(F32)).astype(BF)
    return first, second, third


def travel_rows(z, x, y, nodes):
    node = lax.broadcasted_iota(jnp.int32, (NODE_COLS, LANES), 0)
    node_x = lax.broadcasted_iota(jnp.int32, (NODE_ROWS, LANES), 0).astype(F32)
    scaled = y / SPACING
    cell = jnp.floor(scaled)
    frac = scaled - cell
    cell = cell.astype(jnp.int32)
    x_scaled = x / SPACING
    z_scaled = z / SPACING
    out = []
    for i in range(ROWS):
        hot = jnp.where(node == cell[i : i + 1], 1.0, 0.0).astype(BF)
        hot = jnp.concatenate([hot, hot, hot], axis=0)
        both = jnp.dot(nodes, hot, preferred_element_type=F32)
        count = ND * NODE_ROWS
        along_y = both[:count] + frac[i : i + 1] * both[count:]
        weight_x = jnp.maximum(0.0, 1.0 - jnp.abs(x_scaled[i : i + 1] - node_x))
        z_row = z_scaled[i : i + 1]
        total = None
        for a in range(ND):
            weight_z = jnp.maximum(0.0, 1.0 - jnp.abs(z_row - float(a)))
            term = weight_z * along_y[a * NODE_ROWS : (a + 1) * NODE_ROWS]
            total = term if total is None else total + term
        out.append(jnp.sum(weight_x * total, axis=0, keepdims=True))
    return jnp.concatenate(out, axis=0)


def fill_hats(hats_ref, even, odd, weight_even, weight_odd):
    tiles = HALF // 16
    sample = (
        lax.broadcasted_iota(jnp.int32, (tiles, 16, LANES), 0) * 16
        + lax.broadcasted_iota(jnp.int32, (tiles, 16, LANES), 1)
    ).astype(F32).astype(BF)
    zero = jnp.zeros((), BF)

    def wide(rows, i):
        return jnp.broadcast_to(rows[i : i + 1], (16, LANES)).astype(BF)[None]

    for i in range(ROWS):
        cols = slice(i * LANES, (i + 1) * LANES)
        for half, (index, weight) in enumerate(((even, weight_even), (odd, weight_odd))):
            block = jnp.where(sample == wide(index, i), wide(weight, i), zero)
            hats_ref[half * HALF : (half + 1) * HALF, cols] = block.reshape(HALF, LANES)


def kernel(
    points_ref, nodes_ref, recv_ref, offsets_ref,
    trace_ref, image_ref,
    field, nodes, recv, acc, synth, band, hats, gains, index, weights, picture,
):
    slabs = points_ref.shape[0]
    owners = points_ref.shape[1]
    owned = points_ref.shape[2] // 4
    rows = owned // 2
    chunks = rows // ROWS
    receivers = recv_ref.shape[1]

    for axis in range(2):
        recv[axis] = jnp.broadcast_to(recv_ref[axis], (receivers, LANES))
    synth[...] = jnp.zeros_like(synth)

    def demigrate(slab, _):
        turned = points_ref[slab].T
        for quantity in range(4):
            part = turned[quantity * owned : (quantity + 1) * owned]
            field[quantity] = jnp.concatenate([part[:rows], part[rows:]], axis=1)
        nodes[...] = jnp.concatenate(split3(nodes_ref[slab]), axis=1)
        acc[...] = jnp.zeros_like(acc)

        def step(c, _):
            here = pl.ds(pl.multiple_of(c * ROWS, ROWS), ROWS)
            there = pl.ds(pl.multiple_of(slab * rows + c * ROWS, ROWS), ROWS)
            z, x, y, amplitude = (field[q, here, :] for q in range(4))
            travel = travel_rows(z, x, y, nodes[...])
            first = jnp.floor(travel)
            frac = travel - first
            lower = jnp.floor(first * 0.5)
            is_odd = (first - 2.0 * lower) > 0.5
            even = jnp.where(is_odd, lower + 1.0, lower)
            weight_even = jnp.where(is_odd, frac, 1.0 - frac)
            weight_odd = jnp.where(is_odd, 1.0 - frac, frac)
            index[0, there, :] = even
            index[1, there, :] = lower
            weights[0, there, :] = weight_even
            weights[1, there, :] = weight_odd
            fill_hats(hats, even, lower, amplitude * weight_even, amplitude * weight_odd)
            x_scaled = x * (32.0 / NX)
            y_scaled = y * (32.0 / NX)
            for i in range(ROWS):
                delta_x = recv[0] - x_scaled[i : i + 1]
                delta_y = recv[1] - y_scaled[i : i + 1]
                gain = pl.reciprocal(1.0 + (delta_x * delta_x + delta_y * delta_y), approx=True)
                gains[slab * chunks + c, :, i * LANES : (i + 1) * LANES] = gain.astype(BF)
            acc[...] += lax.dot_general(
                hats[...], gains[slab * chunks + c], (((1,), (1,)), ((), ())),
                preferred_element_type=F32,
            )
            return 0

        lax.fori_loop(0, chunks, step, 0)
        offset = offsets_ref[slab]
        for half in range(2):
            where = pl.ds(offset + half, HALF, stride=2)
            for col in range(0, receivers, LANES):
                part = acc[half * HALF : (half + 1) * HALF, col : col + LANES]
                synth[col // LANES, where, :] += part
        return 0

    lax.fori_loop(0, slabs, demigrate, 0)
    for col in range(0, receivers, LANES):
        trace_ref[col : col + LANES, :] = synth[col // LANES, :SPAN, :].T.astype(BF)

    def migrate(slab, _):
        offset = offsets_ref[slab]
        for half in range(2):
            where = pl.ds(offset + half, HALF, stride=2)
            for col in range(0, receivers, LANES):
                cols = slice(col, col + LANES)
                piece = synth[col // LANES, where, :]
                band[cols, half * HALF : (half + 1) * HALF] = piece.T.astype(BF)

        def step(c, _):
            here = pl.ds(pl.multiple_of(c * ROWS, ROWS), ROWS)
            there = pl.ds(pl.multiple_of(slab * rows + c * ROWS, ROWS), ROWS)
            fill_hats(
                hats, index[0, there, :], index[1, there, :],
                weights[0, there, :], weights[1, there, :],
            )
            product = jnp.dot(band[...], hats[...], preferred_element_type=F32)
            product = product * gains[slab * chunks + c].astype(F32)
            summed = jnp.sum(product, axis=0, keepdims=True)
            picture[here, :] = jnp.concatenate(
                [summed[:, i * LANES : (i + 1) * LANES] for i in range(ROWS)], axis=0
            )
            return 0

        lax.fori_loop(0, chunks, step, 0)
        whole = picture[...] * (1.0 / receivers)
        turned = jnp.concatenate([whole[:, :owners], whole[:, owners:]], axis=0).T
        image_ref[slab, :, :owned] = turned
        image_ref[slab, :, owned:] = jnp.zeros((owners, LANES - owned), F32)
        return 0

    lax.fori_loop(0, slabs, migrate, 0)


def body(
    amplitudes,
    depth_cells,
    lateral_cells,
    jitter,
    tables,
    shot_cells,
    receiver_offsets,
    band_offsets,
):
    owned = amplitudes.shape[1]
    owners = lax.axis_size("shot")
    slabs = lax.axis_size("slab")
    receivers = receiver_offsets.shape[1]
    me = lax.axis_index("slab")

    local = jnp.concatenate(
        [
            depth_cells[0].astype(F32) + jitter[0, 0],
            lateral_cells[0, 0].astype(F32) + jitter[1, 0],
            lateral_cells[1, 0].astype(F32) + jitter[2, 0],
            amplitudes[0],
        ]
    )
    swaps = [[(i, i ^ b) for i in range(slabs)] for b in range(slabs)]

    def swap(array, b):
        return array if b == 0 else lax.ppermute(array, "slab", swaps[b])

    def pick(array, b, axis=0):
        return lax.dynamic_index_in_dim(array, me ^ b, axis, keepdims=False)

    table = jnp.stack([swap(pick(tables[:, 0, :], b), b) for b in range(slabs)])
    table = table.reshape(slabs, ND, NL, NL)
    ahead = jnp.concatenate([table[..., 1:], table[..., -1:]], axis=-1)
    nodes = jnp.stack([table, ahead - table], axis=1)
    nodes = jnp.pad(nodes, ((0, 0), (0, 0), (0, 0), (0, NODE_ROWS - NL), (0, NODE_COLS - NL)))
    nodes = nodes.reshape(slabs, 2 * ND * NODE_ROWS, NODE_COLS)
    offsets = jnp.stack([pick(band_offsets, b) for b in range(slabs)])
    recv = (pick(shot_cells, 0, 1)[:, None] + receiver_offsets).astype(F32) * (32.0 / NX)

    mine = lax.all_to_all(
        jnp.broadcast_to(local[None], (owners, local.shape[0])), "shot", 0, 0
    )
    points = jnp.stack([swap(mine, b) for b in range(slabs)])

    rows = owned // 2
    chunks = rows // ROWS
    vmem = pl.BlockSpec(memory_space=pltpu.VMEM)
    smem = pl.BlockSpec(memory_space=pltpu.SMEM)
    trace, image = pl.pallas_call(
        kernel,
        out_shape=[
            jax.ShapeDtypeStruct((receivers, SPAN), BF),
            jax.ShapeDtypeStruct((slabs, owners, LANES), F32),
        ],
        in_specs=[vmem, vmem, vmem, smem],
        out_specs=[vmem, vmem],
        scratch_shapes=[
            pltpu.VMEM((4, rows, LANES), F32),
            pltpu.VMEM((2 * ND * NODE_ROWS, 3 * NODE_COLS), BF),
            pltpu.VMEM((2, receivers, LANES), F32),
            pltpu.VMEM((BAND, receivers), F32),
            pltpu.VMEM((receivers // LANES, NT, LANES), F32),
            pltpu.VMEM((receivers, BAND), BF),
            pltpu.VMEM((BAND, CHUNK), BF),
            pltpu.VMEM((slabs * chunks, receivers, CHUNK), BF),
            pltpu.VMEM((2, slabs * rows, LANES), F32),
            pltpu.VMEM((2, slabs * rows, LANES), F32),
            pltpu.VMEM((rows, LANES), F32),
        ],
        compiler_params=pltpu.CompilerParams(vmem_limit_bytes=40 * 1024 * 1024),
    )(points, nodes, recv[:, :, None], offsets)

    traces = lax.all_gather(trace, "slab", axis=0)
    synthetic = jnp.pad(traces.astype(F32), ((0, 0), (0, 0), (0, NT - SPAN)))

    part = sum(swap(image[b], b) for b in range(slabs))
    spread = lax.all_to_all(part, "shot", 0, 0)
    return (synthetic, jnp.sum(spread, axis=0)[None, :owned])


def solution(mesh):
    placed = (
        P("slab", "shot"),
        P("slab", "shot"),
        P(None, "slab", "shot"),
        P(None, "slab", "shot"),
        P("shot", "slab", None),
        P(None, "shot"),
        P(),
        P(),
    )
    return jax.shard_map(
        body,
        mesh=mesh,
        in_specs=placed,
        out_specs=(P("shot", None, None), P("slab", "shot")),
        check_vma=False,
    )
```

time: 836 us -> 124 us (0.15)
  the two profiles are of different devices: /device:TPU:2 before, /device:TPU:1 now
where the time goes in v1:
time: 124 us; the launch traced here: 123 us
  Pallas kernels  41.2 us (33%)
  starting transfers between devices  23.2 us (19%)
  blocking collectives  17.5 us (14%)
  between operations  14.2 us (11%)
  waiting for transfers between devices  12.2 us (10%)
  other arithmetic  9.7 us (8%)
  local copies, waits for them, and re-layouts  5.31 us (4%)
    pallas_call x1, Pallas kernels, body(): pl.pallas_call(kernel, out_shape=[jax.ShapeDtypeStruct((receivers, SPAN),...  41.2 us
    all_to_all x1, blocking collectives, body(): spread = lax.all_to_all(part, 'shot', 0, 0)  17.5 us
    all_to_all x1, starting transfers between devices, body(): lax.all_to_all(jnp.broadcast_to(local[None], (owners, local.shape[0])), '...  12.6 us
    ppermute x9, starting transfers between devices, swap(): return array if b == 0 else lax.ppermute(array, 'slab', swaps[b])  10.6 us
    ppermute x9, waiting for transfers between devices, swap(): return array if b == 0 else lax.ppermute(array, 'slab', swaps[b])  6.66 us
    all_to_all x1, waiting for transfers between devices, body(): lax.all_to_all(jnp.broadcast_to(local[None], (owners, local.shape[0])), '...  4.33 us
    pad x1, other arithmetic, body(): synthetic = jnp.pad(traces.astype(F32), ((0, 0), (0, 0), (0, NT - SPAN)))  3.98 us
    another operation x1, other arithmetic, body(): offsets = jnp.stack([pick(band_offsets, b) for b in range(slabs)])  2.58 us
  transfers between devices with their start and end apart: 11, of which 5 were waited for; matrix products, arithmetic and copies ran while one was open for 8% of the time, Pallas kernels for 0%

profile of v1, /device:TPU:1, one launch (start us, length us, event | category | flops | bytes accessed | tf_op | source)
XLA Modules:
  0.0 123.4 jit_solution(13552788614197780606)
XLA Ops:
  7.2 0.8 dynamic-slice_reduce_fusion
  8.0 2.7 %collective-permute-start.5 = (f32[867]{0:T(1024)S(1)}, f32[867]{0:T(1024)S(1)}, u32[]{:S(2)}, u32[]{:S(2)}) collective-permute-start(f32[867]{0:T(1024)S(1)} %get-tuple-element.6), channel_id=1, source_target_pairs={{0,3},{1,2},{2,1},{3,0},{4,7},{5,6},{6,5},{7,4},{8,11},{9,10},{10,... | collective-permute-start | bytes 10412 | tf_op jit(solution)/shard_map/ppermute | solution.py:208
  10.7 0.7 collective-permute-start.3
  11.4 1.3 %collective-permute-start.4 = (f32[867]{0:T(1024)S(1)}, f32[867]{0:T(1024)S(1)}, u32[]{:S(2)}, u32[]{:S(2)}) collective-permute-start(f32[867]{0:T(1024)S(1)} %get-tuple-element.9), channel_id=1, source_target_pairs={{0,2},{1,3},{2,0},{3,1},{4,6},{5,7},{6,4},{7,5},{8,10},{9,11},{10,... | collective-permute-start | bytes 10412 | tf_op jit(solution)/shard_map/ppermute | solution.py:208
  12.7 0.7 bitcast_add_fusion.1
  13.3 0.7 add_bitcast_fusion.1
  14.1 0.7 pad_maximum_fusion.1
  14.8 0.7 broadcast_in_dim.6
  15.5 12.6 %all-to-all-start = ((f32[64,1,384]{2,1,0:T(1,128)}), f32[64,1,384]{2,1,0:T(1,128)S(1)}, u32[]{:S(2)}, u32[]{:S(2)}) async-start(f32[64,1,384]{2,1,0:T(1,128)} %broadcast_in_dim.6), calls=%async_computation | async-start | bytes 196608 | tf_op jit(solution)/shard_map/all_to_all | solution.py:222
  28.2 0.1 stack.56
  28.3 0.2 fusion.2
  28.5 1.5 %fusion.3 = (s32[1]{0:T(128)}, s32[1]{0:T(128)}, s32[1]{0:T(128)}, s32[1]{0:T(128)}) fusion(s32[4]{0:T(128)} %param.15, s32[]{:T(128)S(6)} %select_n.20, s32[]{:T(128)S(6)} %select_n.21, s32[]{:T(128)S(6)} %select_n.23, s32[]{:T(128)S(6)} %select_n.22), kind=kLoop, calls=%fused_computation.36 | loop fusion | bytes 48 | tf_op jit(solution)/shard_map/jit(dynamic_index_in_dim)/dynamic_slice | solution.py:211
  30.0 0.8 multiply_bitcast_fusion
  30.7 2.6 %pad_add_fusion.offsets_ref = s32[4]{0:T(128)S(1)} fusion(s32[1]{0:T(128)} %get-tuple-element.19, s32[1]{0:T(128)} %get-tuple-element.20, s32[1]{0:T(128)} %get-tuple-element.18, s32[1]{0:T(128)} %get-tuple-element.17), kind=kLoop, calls=%fused_computation.31 | loop fusion | flops 12 | bytes 32 | tf_op jit(solution)/shard_map/stack | solution.py:219
  33.3 0.1 copy.16.recv_ref
  34.1 0.2 copy.14
  34.3 0.2 copy.15
  34.4 0.1 stack.57
  34.9 4.3 %all-to-all-done = f32[64,1,384]{2,1,0:T(1,128)S(1)} async-done(((f32[64,1,384]{2,1,0:T(1,128)}), f32[64,1,384]{2,1,0:T(1,128)S(1)}, u32[]{:S(2)}, u32[]{:S(2)}) %all-to-all-start) | async-done | bytes 98336 | tf_op jit(solution)/shard_map/all_to_all | solution.py:222
  39.3 0.4 collective-permute-start.1
  39.7 2.5 %collective-permute-start = (f32[64,384]{1,0:T(8,128)S(1)}, f32[64,384]{1,0:T(8,128)S(1)}, u32[]{:S(2)}, u32[]{:S(2)}) collective-permute-start(f32[64,384]{1,0:T(8,128)S(1)} %bitcast.44), channel_id=1, source_target_pairs={{0,1},{1,0},{2,3},{3,2},{4,5},{5,4},{6,7},{7,6},{8,9},{9,8},{10,11... | collective-permute-start | bytes 294920 | tf_op jit(solution)/shard_map/ppermute | solution.py:208
  42.2 1.0 collective-permute-start.2
  43.3 4.3 %collective-permute-done.2 = f32[64,384]{1,0:T(8,128)S(1)} collective-permute-done((f32[64,384]{1,0:T(8,128)S(1)}, f32[64,384]{1,0:T(8,128)S(1)}, u32[]{:S(2)}, u32[]{:S(2)}) %collective-permute-start.2) | collective-permute-done | bytes 98336 | tf_op jit(solution)/shard_map/ppermute | solution.py:208
  47.6 41.2 %shard_map.95 = (bf16[256,768]{1,0:T(8,128)(2,1)}, f32[4,64,128]{2,1,0:T(8,128)S(1)}) custom-call(f32[4,64,384]{2,1,0:T(8,128)S(1)} %pad_maximum_fusion.points_ref, f32[4,144,32]{2,1,0:T(8,128)S(1)} %bitcast.41, f32[2,256,1]{2,1,0:T(8,128)S(1)} %copy.16.recv_ref, s32[4]{0:T(128)S(1)} %pad_add_fusion.offsets_ref), custom_call_target="tpu_custom_call" | custom-call | tf_op jit(solution)/shard_map/pallas_call | solution.py:231
  89.0 0.7 collective-permute-start.8
  89.7 1.2 collective-permute-start.7
  90.9 1.9 %collective-permute-done.8 = f32[64,128]{1,0:T(8,128)S(1)} collective-permute-done((f32[64,128]{1,0:T(8,128)S(1)}, f32[64,128]{1,0:T(8,128)S(1)}, u32[]{:S(2)}, u32[]{:S(2)}) %collective-permute-start.8) | collective-permute-done | bytes 32800 | tf_op jit(solution)/shard_map/ppermute | solution.py:208
  92.8 0.4 collective-permute-done.7
  93.2 17.5 %all_to_all.18 = f32[64,1,128]{2,1,0:T(1,128)S(1)} all-to-all(f32[64,1,128]{2,1,0:T(1,128)S(1)} %bitcast.47), channel_id=1, replica_groups=mesh['shot'=64,'slab'=4] {'shot'}, dimensions={0} | all-to-all | bytes 65536 | tf_op jit(solution)/shard_map/all_to_all | solution.py:259
  110.8 0.5 slice_bitcast_fusion.4
  111.3 1.2 %all-gather.3.cloned.1.call-done = bf16[1024,768]{1,0:T(8,128)(2,1)} async-done(((bf16[256,768]{1,0:T(8,128)(2,1)}), bf16[1024,768]{1,0:T(8,128)(2,1)}) %all-gather.3.cloned.1.call-update) | async-done | bytes 1572880 | tf_op jit(solution)/shard_map/all_gather | solution.py:255
  112.5 4.0 %pad_convert_fusion = f32[4,256,1024]{2,1,0:T(8,128)} fusion(bf16[4,256,768]{2,1,0:T(8,128)(2,1)} %bitcast.42), kind=kLoop, calls=%fused_computation | loop fusion | flops 1048576 | bytes 5767168 | tf_op jit(solution)/shard_map/jit(_pad)/pad | solution.py:256
  (34 shorter events, 1.4 us)
Async XLA Ops:
  7.2 21.2 %copy-start = (s32[2,4]{1,0:T(2,128)S(1)}, s32[2,4]{1,0:T(2,128)}, u32[]{:S(2)}) copy-start(s32[2,4]{1,0:T(2,128)} %param.13) | copy-start | bytes 100
  8.0 25.8 %collective-permute-start.5 = (f32[867]{0:T(1024)S(1)}, f32[867]{0:T(1024)S(1)}, u32[]{:S(2)}, u32[]{:S(2)}) collective-permute-start(f32[867]{0:T(1024)S(1)} %get-tuple-element.6), channel_id=1, source_target_pairs={{0,3},{1,2},{2,1},{3,0},{4,7},{5,6},{6,5},{7,4},{8,11},{9,10},{10,... | collective-permute-start | bytes 10412 | tf_op jit(solution)/shard_map/ppermute | solution.py:208
  10.7 22.8 %collective-permute-start.3 = (f32[867]{0:T(1024)S(1)}, f32[867]{0:T(1024)S(1)}, u32[]{:S(2)}, u32[]{:S(2)}) collective-permute-start(f32[867]{0:T(1024)S(1)} %get-tuple-element.7), channel_id=1, source_target_pairs={{0,1},{1,0},{2,3},{3,2},{4,5},{5,4},{6,7},{7,6},{8,9},{9,8},{10,11... | collective-permute-start | bytes 10412 | tf_op jit(solution)/shard_map/ppermute | solution.py:208
  11.4 22.2 %collective-permute-start.4 = (f32[867]{0:T(1024)S(1)}, f32[867]{0:T(1024)S(1)}, u32[]{:S(2)}, u32[]{:S(2)}) collective-permute-start(f32[867]{0:T(1024)S(1)} %get-tuple-element.9), channel_id=1, source_target_pairs={{0,2},{1,3},{2,0},{3,1},{4,6},{5,7},{6,4},{7,5},{8,10},{9,11},{10,... | collective-permute-start | bytes 10412 | tf_op jit(solution)/shard_map/ppermute | solution.py:208
  15.5 23.8 %all-to-all-start = ((f32[64,1,384]{2,1,0:T(1,128)}), f32[64,1,384]{2,1,0:T(1,128)S(1)}, u32[]{:S(2)}, u32[]{:S(2)}) async-start(f32[64,1,384]{2,1,0:T(1,128)} %broadcast_in_dim.6), calls=%async_computation | async-start | bytes 196608 | tf_op jit(solution)/shard_map/all_to_all | solution.py:222
  28.0 84.5 %all-gather.3.cloned.1.call-start = ((), (), s32[]{:S(2)}) async-start(), calls=%async_computation.2 | async-start | bytes 1966080 | tf_op jit(solution)/shard_map/all_gather | solution.py:255
  39.3 4.0 %collective-permute-start.1 = (f32[64,384]{1,0:T(8,128)S(1)}, f32[64,384]{1,0:T(8,128)S(1)}, u32[]{:S(2)}, u32[]{:S(2)}) collective-permute-start(f32[64,384]{1,0:T(8,128)S(1)} %bitcast.43), channel_id=1, source_target_pairs={{0,2},{1,3},{2,0},{3,1},{4,6},{5,7},{6,4},{7,5},{8,10},{9,11},{10,... | collective-permute-start | bytes 294920 | tf_op jit(solution)/shard_map/ppermute | solution.py:208
  39.7 3.6 %collective-permute-start = (f32[64,384]{1,0:T(8,128)S(1)}, f32[64,384]{1,0:T(8,128)S(1)}, u32[]{:S(2)}, u32[]{:S(2)}) collective-permute-start(f32[64,384]{1,0:T(8,128)S(1)} %bitcast.44), channel_id=1, source_target_pairs={{0,1},{1,0},{2,3},{3,2},{4,5},{5,4},{6,7},{7,6},{8,9},{9,8},{10,11... | collective-permute-start | bytes 294920 | tf_op jit(solution)/shard_map/ppermute | solution.py:208
  42.2 5.4 %collective-permute-start.2 = (f32[64,384]{1,0:T(8,128)S(1)}, f32[64,384]{1,0:T(8,128)S(1)}, u32[]{:S(2)}, u32[]{:S(2)}) collective-permute-start(f32[64,384]{1,0:T(8,128)S(1)} %bitcast.45), channel_id=1, source_target_pairs={{0,3},{1,2},{2,1},{3,0},{4,7},{5,6},{6,5},{7,4},{8,11},{9,10},{10,... | collective-permute-start | bytes 294920 | tf_op jit(solution)/shard_map/ppermute | solution.py:208
  88.9 2.0 %collective-permute-start.6 = (f32[64,128]{1,0:T(8,128)S(1)}, f32[64,128]{1,0:T(8,128)S(1)}, u32[]{:S(2)}, u32[]{:S(2)}) collective-permute-start(f32[64,128]{1,0:T(8,128)S(1)} %get-tuple-element.10), channel_id=1, source_target_pairs={{0,1},{1,0},{2,3},{3,2},{4,5},{5,4},{6,7},{7,6},{8,9},{9,8},{10,11... | collective-permute-start | bytes 98312 | tf_op jit(solution)/shard_map/ppermute | solution.py:208
  89.0 3.8 %collective-permute-start.8 = (f32[64,128]{1,0:T(8,128)S(1)}, f32[64,128]{1,0:T(8,128)S(1)}, u32[]{:S(2)}, u32[]{:S(2)}) collective-permute-start(f32[64,128]{1,0:T(8,128)S(1)} %get-tuple-element.11), channel_id=1, source_target_pairs={{0,3},{1,2},{2,1},{3,0},{4,7},{5,6},{6,5},{7,4},{8,11},{9,10},{10,... | collective-permute-start | bytes 98312 | tf_op jit(solution)/shard_map/ppermute | solution.py:208
  89.7 3.5 %collective-permute-start.7 = (f32[64,128]{1,0:T(8,128)S(1)}, f32[64,128]{1,0:T(8,128)S(1)}, u32[]{:S(2)}, u32[]{:S(2)}) collective-permute-start(f32[64,128]{1,0:T(8,128)S(1)} %get-tuple-element.12), channel_id=1, source_target_pairs={{0,2},{1,3},{2,0},{3,1},{4,6},{5,7},{6,4},{7,5},{8,10},{9,11},{10,... | collective-permute-start | bytes 98312 | tf_op jit(solution)/shard_map/ppermute | solution.py:208
Sparse Core Ops, SparseCore 0:
  89.0 23.4 all-gather.2

commit v2 on v0

v2 whole, which is shorter than its diff:
```python
import functools

import jax
import jax.numpy as jnp
from jax import lax
from jax.experimental import pallas as pl
from jax.experimental.pallas import tpu as pltpu
from jax.sharding import PartitionSpec as P

NX = 512
NT = 1024
BAND = 512
HALF = 256
SPACING = 32
NL = 17
ND = 3
SPAN = 768
LANES = 128
SEGMENTS = 3
ROWS = 8
MXU = 256
PIECE = 16
BF = jnp.bfloat16
F32 = jnp.float32


def travel_octet(z, x, y, table):
    x_scaled = x / SPACING
    z_scaled = z / SPACING
    y_scaled = y / SPACING
    x_cell = jnp.floor(x_scaled)
    y_cell = jnp.floor(y_scaled)
    x_part = x_scaled - x_cell
    y_part = y_scaled - y_cell
    node = (x_cell * NL + y_cell).astype(jnp.int32)
    total = jnp.zeros_like(z)
    corner_weights = ((1.0 - x_part, x_part), (1.0 - y_part, y_part))
    plane_weights = [jnp.maximum(0.0, 1.0 - jnp.abs(z_scaled - float(a))) for a in range(ND)]
    for b in range(2):
        for c in range(2):
            at = node + (b * NL + c)
            lane = at & (LANES - 1)
            block = at >> 7
            first, second = block == 0, block == 1
            value = jnp.zeros_like(z)
            for a in range(ND):
                found = [
                    jnp.take_along_axis(
                        jnp.broadcast_to(table[SEGMENTS * a + k : SEGMENTS * a + k + 1], z.shape),
                        lane, axis=1, mode="promise_in_bounds",
                    )
                    for k in range(SEGMENTS)
                ]
                picked = jnp.where(first, found[0], jnp.where(second, found[1], found[2]))
                value = value + plane_weights[a] * picked
                yield
            total = total + (corner_weights[0][b] * corner_weights[1][c]) * value
    return total


def interleave(*works):
    works = list(works)
    while works:
        for work in list(works):
            if next(work, works) is works:
                works.remove(work)


def kernel(
    points_ref, nodes_ref, recv_ref, offsets_ref,
    trace_ref, image_ref,
    field, recv, synth, band, gains, index, picture,
    near0, near1, *push,
):
    slabs = points_ref.shape[0]
    owners = points_ref.shape[1]
    owned = points_ref.shape[2] // 4
    rows = owned // 2
    steps = rows // ROWS
    receivers = recv_ref.shape[1]
    part = PIECE
    pieces = BAND // part
    near = (near0, near1)

    for k in range(3):
        recv[k] = jnp.broadcast_to(recv_ref[k], (receivers, LANES))
    synth[...] = jnp.zeros_like(synth)
    for slab in range(slabs):
        turned = points_ref[slab].T
        for quantity in range(4):
            piece = turned[quantity * owned : (quantity + 1) * owned]
            field[quantity, slab * rows : (slab + 1) * rows] = jnp.concatenate(
                [piece[:rows], piece[rows:]], axis=1
            )

    def octet(c):
        return pl.ds(pl.multiple_of(c * ROWS, ROWS), ROWS)

    def locate(c, slab, slot):
        z, x, y, amplitude = (field[q, octet(c), :] for q in range(4))
        travel = yield from travel_octet(z, x, y, nodes_ref[slab])
        first = jnp.floor(travel)
        frac = travel - first
        lower = jnp.floor(first * 0.5)
        is_odd = (first - 2.0 * lower) > 0.5
        even = jnp.where(is_odd, lower + 1.0, lower)
        weight_even = jnp.where(is_odd, frac, 1.0 - frac)
        weight_odd = jnp.where(is_odd, 1.0 - frac, frac)
        for k, value in enumerate((even, lower, weight_even, weight_odd)):
            index[k, octet(c), :] = value
        x_near = (x - offsets_ref[slabs]) * (32.0 / NX)
        y_near = (y - offsets_ref[slabs + 1]) * (32.0 / NX)
        square = x_near * x_near + y_near * y_near
        ready = (
            even, lower, amplitude * weight_even, amplitude * weight_odd, x_near, y_near, square
        )
        for k, value in enumerate(ready):
            near[slot][k] = value
        yield

    def radiate(c, pair, slot):
        group = (2 * pair, 2 * pair + 1)
        x_near, y_near, square = (
            [jnp.broadcast_to(near[slot][k, i : i + 1, :], (8, LANES)) for i in group]
            for k in range(4, 7)
        )
        for block in range(0, receivers, 16):
            at = [slice(block + 8 * h, block + 8 * h + 8) for h in range(2)]
            base = [[recv[k, at[h], :] for h in range(2)] for k in range(3)]
            for k, i in enumerate(group):
                gain = jnp.concatenate(
                    [
                        pl.reciprocal(
                            (base[0][h] + square[k])
                            - (base[1][h] * x_near[k] + base[2][h] * y_near[k]),
                            approx=True,
                        )
                        for h in range(2)
                    ],
                    axis=0,
                ).astype(BF)
                gains[c * ROWS + i, block : block + 16, :] = gain
                push[pair][k, block : block + 16, :] = gain
            yield
    def stack(pair, slot, sums):
        group = (2 * pair, 2 * pair + 1)
        pltpu.matmul_push_rhs(
            jnp.concatenate([push[pair][k] for k in range(2)], axis=1),
            pair // 2, pair % 2, transpose=True,
        )
        wide = [
            [jnp.broadcast_to(near[slot][k, i : i + 1, :], (16, LANES)).astype(BF) for i in group]
            for k in range(4)
        ]
        for tile in range(0, HALF, 16):
            sample = (lax.broadcasted_iota(jnp.int32, (16, LANES), 0) + tile).astype(F32).astype(BF)
            for half in range(2):
                hat = [
                    jnp.where(sample == wide[half][k], wide[2 + half][k], jnp.zeros((), BF))
                    for k in range(2)
                ]
                pltpu.matmul_acc_lhs(
                    sums[pair % 2][(half * HALF + tile) // part], jnp.concatenate(hat, axis=1),
                    load_staged_rhs=pair // 2 if tile == 0 and half == 0 else None,
                )
            yield

    def demigrate(*accumulators):
        sums = (accumulators[:pieces], accumulators[pieces:])
        last = slabs * steps - 1

        def phase(c, slot):
            ahead = jnp.minimum(c + 1, last)
            interleave(
                stack(0, slot, sums), stack(1, slot, sums),
                radiate(c, 2, slot), radiate(c, 3, slot),
                locate(ahead, ahead // steps, 1 - slot),
            )
            interleave(
                stack(2, slot, sums), stack(3, slot, sums),
                radiate(ahead, 0, 1 - slot), radiate(ahead, 1, 1 - slot),
            )

        def one_slab(slab, _):
            def two(j, _):
                c = slab * steps + 2 * j
                phase(c, 0)
                phase(c + 1, 1)
                return 0

            lax.fori_loop(0, steps // 2, two, 0)
            offset = offsets_ref[slab]
            for k in range(pieces):
                total = pltpu.matmul_pop(sums[0][k]) + pltpu.matmul_pop(sums[1][k])
                half, start = divmod(k * part, HALF)
                where = pl.ds(offset + half + 2 * start, part, stride=2)
                for col in range(0, receivers, LANES):
                    synth[col // LANES, where, :] += total[:, col : col + LANES]
            return 0

        interleave(locate(0, 0, 0))
        interleave(radiate(0, 0, 0), radiate(0, 1, 0))
        lax.fori_loop(0, slabs, one_slab, 0)

    pl.run_scoped(
        demigrate,
        *[pltpu.ACC(mxu_id=unit)((part, MXU), F32) for unit in range(2) for _ in range(pieces)],
    )

    for col in range(0, receivers, LANES):
        trace_ref[col : col + LANES, :] = synth[col // LANES, :SPAN, :].T.astype(BF)
    for slab in range(slabs):
        offset = offsets_ref[slab]
        for half in range(2):
            where = pl.ds(offset + half, HALF, stride=2)
            for col in range(receivers // LANES):
                band[slab, col, half * HALF : (half + 1) * HALF, :] = synth[col, where, :].astype(BF)

    def migrate(*accumulators):
        groups = [accumulators[g * pieces : (g + 1) * pieces] for g in range(4)]
        sums = (groups[:2], groups[2:])
        sample = lax.broadcasted_iota(jnp.int32, (8, LANES), 0).astype(F32)

        def correlate(c, pair):
            unit, group = pair % 2, pair // 2
            slab = c // steps
            rhs = [gains[c * ROWS + 2 * pair + k] for k in range(2)]
            pltpu.matmul_push_rhs(jnp.concatenate(rhs, axis=1), group, unit)
            yield
            for k in range(pieces):
                lhs = [band[slab, col, k * part : (k + 1) * part, :] for col in range(2)]
                pltpu.matmul_acc_lhs(
                    sums[unit][group][k], jnp.concatenate(lhs, axis=1),
                    load_staged_rhs=group if k == 0 else None,
                )
                yield

        def collect(c, pair):
            unit, group = pair % 2, pair // 2
            found = [[jnp.zeros((8, LANES), F32) for _ in range(2)] for _ in range(2)]
            rows8 = [[index[k, octet(c), :][2 * pair + i : 2 * pair + i + 1] for i in range(2)] for k in range(4)]
            wide = [[jnp.broadcast_to(rows8[k][i], (8, LANES)) for i in range(2)] for k in range(2)]
            for k in range(pieces):
                popped = pltpu.matmul_pop(sums[unit][group][k])
                half, start = divmod(k * part, HALF)
                for block in range(part // 8):
                    here = sample + float(start + block * 8)
                    for i in range(2):
                        value = popped[block * 8 : (block + 1) * 8, i * LANES : (i + 1) * LANES]
                        found[half][i] = jnp.where(here == wide[half][i], value, found[half][i])
                yield
            for i in range(2):
                both = sum(
                    found[half][i] * rows8[2 + half][i].astype(BF).astype(F32) for half in range(2)
                )
                row = 2 * pair + i
                picture[c, row : row + 1, :] = jnp.sum(both, axis=0, keepdims=True)
            yield

        count = slabs * steps

        def step(c, _):
            interleave(correlate(c, 0), correlate(c, 1), collect(c - 1, 2), collect(c - 1, 3))
            interleave(correlate(c, 2), correlate(c, 3), collect(c, 0), collect(c, 1))
            return 0

        interleave(correlate(0, 0), correlate(0, 1))
        interleave(correlate(0, 2), correlate(0, 3), collect(0, 0), collect(0, 1))
        lax.fori_loop(1, count, step, 0)
        interleave(collect(count - 1, 2), collect(count - 1, 3))

    pl.run_scoped(
        migrate,
        *[pltpu.ACC(mxu_id=unit)((part, MXU), F32) for unit in range(2) for _ in range(2 * pieces)],
    )
    for slab in range(slabs):
        whole = picture[slab * steps : (slab + 1) * steps].reshape(rows, LANES) * (1.0 / receivers)
        turned = jnp.concatenate([whole[:, :owners], whole[:, owners:]], axis=0).T
        turned = jnp.concatenate([turned, jnp.zeros((owners, LANES - owned), F32)], axis=1)
        image_ref[pl.ds(offsets_ref[slabs + 2 + slab], owners, stride=slabs), :] = turned


def pack(amplitudes_ref, depth_ref, lateral_ref, jitter_ref, out_ref):
    row = jnp.concatenate(
        [
            depth_ref[...].astype(F32) + jitter_ref[0],
            lateral_ref[0].astype(F32) + jitter_ref[1],
            lateral_ref[1].astype(F32) + jitter_ref[2],
            amplitudes_ref[...],
        ],
        axis=1,
    )
    out_ref[...] = jnp.broadcast_to(row[None], out_ref.shape)


def probe(points, nodes, recv, offsets):
    slabs, owners, width = points.shape
    owned = width // 4
    rows = owned // 2
    receivers = recv.shape[1]
    vmem = pl.BlockSpec(memory_space=pltpu.VMEM)
    smem = pl.BlockSpec(memory_space=pltpu.SMEM)
    return pl.pallas_call(
        kernel,
        out_shape=[
            jax.ShapeDtypeStruct((receivers, SPAN), BF),
            jax.ShapeDtypeStruct((owners * slabs, LANES), F32),
        ],
        in_specs=[vmem, vmem, vmem, smem],
        out_specs=[vmem, vmem],
        scratch_shapes=[
            pltpu.VMEM((4, slabs * rows, LANES), F32),
            pltpu.VMEM((3, receivers, LANES), F32),
            pltpu.VMEM((receivers // LANES, NT, LANES), F32),
            pltpu.VMEM((slabs, receivers // LANES, BAND, LANES), BF),
            pltpu.VMEM((slabs * rows, receivers, LANES), BF),
            pltpu.VMEM((4, slabs * rows, LANES), F32),
            pltpu.VMEM((slabs * rows // ROWS, ROWS, LANES), F32),
            *[pltpu.VMEM((7, ROWS, LANES), F32) for _ in range(2)],
            *[pltpu.VMEM((2, receivers, LANES), BF) for _ in range(ROWS // 2)],
        ],
        compiler_params=pltpu.CompilerParams(vmem_limit_bytes=48 * 1024 * 1024),
    )(points, nodes, recv, offsets)


def body(
    amplitudes,
    depth_cells,
    lateral_cells,
    jitter,
    tables,
    shot_cells,
    receiver_offsets,
    band_offsets,
):
    owned = amplitudes.shape[1]
    owners = lax.axis_size("shot")
    slabs = lax.axis_size("slab")
    receivers = receiver_offsets.shape[1]
    me = lax.axis_index("slab")

    local = pl.pallas_call(
        pack, out_shape=jax.ShapeDtypeStruct((owners, 1, 4 * owned), F32)
    )(amplitudes, depth_cells, lateral_cells, jitter)
    swaps = [[(i, i ^ b) for i in range(slabs)] for b in range(slabs)]

    def swap(array, b):
        return array if b == 0 else lax.ppermute(array, "slab", swaps[b])

    def pick(array, b, axis=0):
        return lax.dynamic_index_in_dim(array, me ^ b, axis, keepdims=False)

    table = jnp.stack([swap(pick(tables[:, 0, :], b), b) for b in range(slabs)])
    nodes = jnp.pad(
        table.reshape(slabs, ND, NL * NL), ((0, 0), (0, 0), (0, SEGMENTS * LANES - NL * NL))
    ).reshape(slabs, ND * SEGMENTS, LANES)
    shot = pick(shot_cells, 0, 1)
    places = me ^ jnp.arange(slabs, dtype=jnp.int32)
    offsets = jnp.concatenate(
        [jnp.stack([pick(band_offsets, b) for b in range(slabs)]), shot, places]
    )
    near = receiver_offsets.astype(F32) * (32.0 / NX)
    recv = jnp.stack([1.0 + near[0] * near[0] + near[1] * near[1], 2.0 * near[0], 2.0 * near[1]])

    mine = lax.all_to_all(local, "shot", 0, 0)[:, 0]
    points = jnp.stack([swap(mine, b) for b in range(slabs)])

    trace, image = probe(points, nodes, recv[:, :, None], offsets)

    spread = lax.all_to_all(image, ("shot", "slab"), 0, 0)

    near_trace = swap(trace, 1)
    far_trace = swap(trace, 2)
    last_trace = swap(far_trace, 1)
    odd, upper = me % 2 == 1, me >= 2

    def ordered(flag, first, second):
        return jnp.where(flag, second, first), jnp.where(flag, first, second)

    low = ordered(odd, trace, near_trace)
    high = ordered(odd, far_trace, last_trace)
    first, third = ordered(upper, low[0], high[0])
    second, fourth = ordered(upper, low[1], high[1])
    synthetic = jnp.pad(
        jnp.stack([first, second, third, fourth]).astype(F32), ((0, 0), (0, 0), (0, NT - SPAN))
    )
    return (synthetic, jnp.sum(spread, axis=0)[None, :owned])


def solution(mesh):
    placed = (
        P("slab", "shot"),
        P("slab", "shot"),
        P(None, "slab", "shot"),
        P(None, "slab", "shot"),
        P("shot", "slab", None),
        P(None, "shot"),
        P(),
        P(),
    )
    return jax.shard_map(
        body,
        mesh=mesh,
        in_specs=placed,
        out_specs=(P("shot", None, None), P("slab", "shot")),
        check_vma=False,
    )
```

time: 836 us -> 88.4 us (0.11)
  the two profiles are of different devices: /device:TPU:2 before, /device:TPU:1 now
where the time goes in v2:
time: 88.4 us; the launch traced here: 88.1 us
  starting transfers between devices  30.6 us (35%)
  Pallas kernels  26.8 us (30%)
  waiting for transfers between devices  20.1 us (23%)
  local copies, waits for them, and re-layouts  6.08 us (7%)
  other arithmetic  3.74 us (4%)
    pallas_call x1, Pallas kernels, probe(): pl.pallas_call(kernel, out_shape=[jax.ShapeDtypeStruct((receivers, SPAN),...  25.4 us
    all_to_all x1, starting transfers between devices, body(): mine = lax.all_to_all(local, 'shot', 0, 0)[:, 0]  12.6 us
    ppermute x9, starting transfers between devices, swap(): return array if b == 0 else lax.ppermute(array, 'slab', swaps[b])  11.8 us
    all_to_all x1, waiting for transfers between devices, body(): spread = lax.all_to_all(image, ('shot', 'slab'), 0, 0)  7.42 us
    ppermute x9, waiting for transfers between devices, swap(): return array if b == 0 else lax.ppermute(array, 'slab', swaps[b])  6.97 us
    all_to_all x1, starting transfers between devices, body(): spread = lax.all_to_all(image, ('shot', 'slab'), 0, 0)  6.2 us
    all_to_all x1, waiting for transfers between devices, body(): mine = lax.all_to_all(local, 'shot', 0, 0)[:, 0]  5.72 us
    concatenate x1, local copies, waits for them, and re-layouts, body(): jnp.concatenate([jnp.stack([pick(band_offsets, b) for b in range(slabs)])...  2.6 us
  transfers between devices with their start and end apart: 11, of which 4 were waited for; matrix products, arithmetic and copies ran while one was open for 7% of the time, Pallas kernels for 2%

profile of v2, /device:TPU:1, one launch (start us, length us, event | category | flops | bytes accessed | tf_op | source)
XLA Modules:
  0.0 88.1 jit_solution(12361228561802507847)
XLA Ops:
  0.6 0.0 copy-start
  0.7 0.8 dynamic-slice_reduce_fusion.3
  1.4 3.3 %collective-permute-start.3 = (f32[867]{0:T(1024)S(1)}, f32[867]{0:T(1024)S(1)}, u32[]{:S(2)}, u32[]{:S(2)}) collective-permute-start(f32[867]{0:T(1024)S(1)} %get-tuple-element.7), channel_id=1, source_target_pairs={{0,1},{1,0},{2,3},{3,2},{4,5},{5,4},{6,7},{7,6},{8,9},{9,8},{10,11... | collective-permute-start | bytes 10412 | tf_op jit(solution)/shard_map/ppermute | solution.py:348
  4.8 1.4 %collective-permute-start.4 = (f32[867]{0:T(1024)S(1)}, f32[867]{0:T(1024)S(1)}, u32[]{:S(2)}, u32[]{:S(2)}) collective-permute-start(f32[867]{0:T(1024)S(1)} %get-tuple-element.9), channel_id=1, source_target_pairs={{0,2},{1,3},{2,0},{3,1},{4,6},{5,7},{6,4},{7,5},{8,10},{9,11},{10,... | collective-permute-start | bytes 10412 | tf_op jit(solution)/shard_map/ppermute | solution.py:348
  6.2 1.5 %shard_map.95 = f32[64,1,384]{2,1,0:T(1,128)} custom-call(f32[1,96]{1,0:T(1,128)} %amplitudes_ref.1, s32[1,96]{1,0:T(1,128)} %depth_ref.1, s32[2,1,96]{2,1,0:T(1,128)} %lateral_ref.1, f32[3,1,96]{2,1,0:T(1,128)} %jitter_ref.1), custom_call_target="tpu_custom_call" | custom-call | tf_op jit(solution)/shard_map/pallas_call | solution.py:342
  7.7 12.6 %all-to-all-start = ((f32[64,1,384]{2,1,0:T(1,128)}), f32[64,1,384]{2,1,0:T(1,128)S(1)}, u32[]{:S(2)}, u32[]{:S(2)}) async-start(f32[64,1,384]{2,1,0:T(1,128)} %shard_map.95), calls=%async_computation | async-start | bytes 196608 | tf_op jit(solution)/shard_map/all_to_all | solution.py:365
  20.3 0.7 convert_multiply_fusion
  21.0 0.2 fusion.8
  21.2 0.1 stack.56
  21.2 0.2 copy.13.recv_ref
  21.4 1.5 %fusion.9 = (s32[1]{0:T(128)}, s32[1]{0:T(128)}, s32[1]{0:T(128)}, s32[1]{0:T(128)}) fusion(s32[4]{0:T(128)} %param.15, s32[]{:T(128)S(6)} %select_n.71, s32[]{:T(128)S(6)} %select_n.69, s32[]{:T(128)S(6)} %select_n.68, s32[]{:T(128)S(6)} %select_n.70), kind=kLoop, calls=%fused_computation.37 | loop fusion | bytes 48 | tf_op jit(solution)/shard_map/jit(dynamic_index_in_dim)/dynamic_slice | solution.py:351
  22.9 2.6 %concatenate.4.offsets_ref = s32[10]{0:T(128)S(1)} concatenate(s32[1]{0:T(128)} %get-tuple-element.21, s32[1]{0:T(128)} %get-tuple-element.20, s32[1]{0:T(128)} %get-tuple-element.22, s32[1]{0:T(128)} %get-tuple-element.19, s32[2]{0:T(128)S(1)} %fusion.8, s32[4]{0:T(128)S(1)} %iota_xor_fusion), dimensions={0} | concatenate | bytes 80 | tf_op jit(solution)/shard_map/concatenate | solution.py:359
  25.5 0.1 stack.57
  25.6 0.1 stack.59
  25.7 0.1 stack.58
  25.8 5.7 %all-to-all-done = f32[64,1,384]{2,1,0:T(1,128)S(1)} async-done(((f32[64,1,384]{2,1,0:T(1,128)}), f32[64,1,384]{2,1,0:T(1,128)S(1)}, u32[]{:S(2)}, u32[]{:S(2)}) %all-to-all-start) | async-done | bytes 98336 | tf_op jit(solution)/shard_map/all_to_all | solution.py:365
  31.5 0.4 collective-permute-start.1
  31.9 2.4 %collective-permute-start = (f32[64,384]{1,0:T(8,128)S(1)}, f32[64,384]{1,0:T(8,128)S(1)}, u32[]{:S(2)}, u32[]{:S(2)}) collective-permute-start(f32[64,384]{1,0:T(8,128)S(1)} %bitcast.24), channel_id=1, source_target_pairs={{0,1},{1,0},{2,3},{3,2},{4,5},{5,4},{6,7},{7,6},{8,9},{9,8},{10,11... | collective-permute-start | bytes 294920 | tf_op jit(solution)/shard_map/ppermute | solution.py:348
  34.3 1.0 %collective-permute-start.2 = (f32[64,384]{1,0:T(8,128)S(1)}, f32[64,384]{1,0:T(8,128)S(1)}, u32[]{:S(2)}, u32[]{:S(2)}) collective-permute-start(f32[64,384]{1,0:T(8,128)S(1)} %bitcast.25), channel_id=1, source_target_pairs={{0,3},{1,2},{2,1},{3,0},{4,7},{5,6},{6,5},{7,4},{8,11},{9,10},{10,... | collective-permute-start | bytes 294920 | tf_op jit(solution)/shard_map/ppermute | solution.py:348
  35.4 0.0 collective-permute-done.1
  35.4 4.3 %collective-permute-done.2 = f32[64,384]{1,0:T(8,128)S(1)} collective-permute-done((f32[64,384]{1,0:T(8,128)S(1)}, f32[64,384]{1,0:T(8,128)S(1)}, u32[]{:S(2)}, u32[]{:S(2)}) %collective-permute-start.2) | collective-permute-done | bytes 98336 | tf_op jit(solution)/shard_map/ppermute | solution.py:348
  39.8 25.4 %shard_map.96 = (bf16[256,768]{1,0:T(8,128)(2,1)S(1)}, f32[256,128]{1,0:T(8,128)}) custom-call(f32[4,64,384]{2,1,0:T(8,128)S(1)} %pad_maximum_fusion.points_ref, f32[4,9,128]{2,1,0:T(8,128)S(1)} %reshape.25.nodes_ref, f32[3,256,1]{2,1,0:T(8,128)S(1)} %copy.13.recv_ref, s32[10]{0:T(128)S(1)} %concatenate.4.offsets_ref), custom_call_target="tpu_custom_call" | custom-call | tf_op jit(solution)/shard_map/pallas_call | solution.py:303
  65.2 0.3 collective-permute-start.6
  65.5 6.2 %all-to-all-start.1 = ((f32[256,1,128]{2,1,0:T(1,128)}), f32[256,1,128]{2,1,0:T(1,128)S(1)}, u32[]{:S(2)}, u32[]{:S(2)}) async-start(f32[256,1,128]{2,1,0:T(1,128)} %bitcast.9), calls=%async_computation.1 | async-start | bytes 262144 | tf_op jit(solution)/shard_map/all_to_all | solution.py:370
  71.7 2.2 %collective-permute-start.8 = (bf16[256,768]{1,0:T(8,128)(2,1)S(1)}, bf16[256,768]{1,0:T(8,128)(2,1)S(1)}, u32[]{:S(2)}, u32[]{:S(2)}) collective-permute-start(bf16[256,768]{1,0:T(8,128)(2,1)S(1)} %get-tuple-element.4), channel_id=1, source_target_pairs={{0,1},{1,0},{2,3},{3,2},{4,5},{5,4},{6,7},{7,6},{8,9},{9,8},{10,11... | collective-permute-start | bytes 1179656 | tf_op jit(solution)/shard_map/ppermute | solution.py:348
  73.9 2.6 %collective-permute-done.6 = bf16[256,768]{1,0:T(8,128)(2,1)S(1)} collective-permute-done((bf16[256,768]{1,0:T(8,128)(2,1)S(1)}, bf16[256,768]{1,0:T(8,128)(2,1)S(1)}, u32[]{:S(2)}, u32[]{:S(2)}) %collective-permute-start.6) | collective-permute-done | bytes 393248 | tf_op jit(solution)/shard_map/ppermute | solution.py:348
  76.5 0.7 collective-permute-start.7
  77.2 7.4 %all-to-all-done.1 = f32[256,1,128]{2,1,0:T(1,128)S(1)} async-done(((f32[256,1,128]{2,1,0:T(1,128)}), f32[256,1,128]{2,1,0:T(1,128)S(1)}, u32[]{:S(2)}, u32[]{:S(2)}) %all-to-all-start.1) | async-done | bytes 131104 | tf_op jit(solution)/shard_map/all_to_all | solution.py:370
  84.6 0.3 reduce_sum.9
  84.9 0.5 slice_bitcast_fusion
  85.4 0.1 select_bitcast_fusion.3
  85.5 2.6 %fusion.7 = f32[4,256,1024]{2,1,0:T(8,128)} fusion(bf16[1,256,768]{2,1,0:T(8,128)(2,1)S(1)} %get-tuple-element.13, bf16[1,256,768]{2,1,0:T(8,128)(2,1)S(1)} %get-tuple-element.12, bf16[1,256,768]{2,1,0:T(8,128)(2,1)S(1)} %get-tuple-element.11, bf16[1,256,768]{2,1,0:T(8,128)(2,1)S(1)} %get-tuple-element.10), kind=kLoop, calls=%fused_computation.8 | loop fusion | flops 13631488 | bytes 5767168 | tf_op jit(solution)/shard_map/jit(_pad)/pad | solution.py:384
  (15 shorter events, 0.1 us)
Async XLA Ops:
  0.6 20.3 %copy-start = (s32[2,4]{1,0:T(2,128)S(1)}, s32[2,4]{1,0:T(2,128)}, u32[]{:S(2)}) copy-start(s32[2,4]{1,0:T(2,128)} %param.13) | copy-start | bytes 100
  1.4 24.1 %collective-permute-start.3 = (f32[867]{0:T(1024)S(1)}, f32[867]{0:T(1024)S(1)}, u32[]{:S(2)}, u32[]{:S(2)}) collective-permute-start(f32[867]{0:T(1024)S(1)} %get-tuple-element.7), channel_id=1, source_target_pairs={{0,1},{1,0},{2,3},{3,2},{4,5},{5,4},{6,7},{7,6},{8,9},{9,8},{10,11... | collective-permute-start | bytes 10412 | tf_op jit(solution)/shard_map/ppermute | solution.py:348
  4.8 20.8 %collective-permute-start.5 = (f32[867]{0:T(1024)S(1)}, f32[867]{0:T(1024)S(1)}, u32[]{:S(2)}, u32[]{:S(2)}) collective-permute-start(f32[867]{0:T(1024)S(1)} %get-tuple-element.8), channel_id=1, source_target_pairs={{0,3},{1,2},{2,1},{3,0},{4,7},{5,6},{6,5},{7,4},{8,11},{9,10},{10,... | collective-permute-start | bytes 10412 | tf_op jit(solution)/shard_map/ppermute | solution.py:348
  4.8 20.9 %collective-permute-start.4 = (f32[867]{0:T(1024)S(1)}, f32[867]{0:T(1024)S(1)}, u32[]{:S(2)}, u32[]{:S(2)}) collective-permute-start(f32[867]{0:T(1024)S(1)} %get-tuple-element.9), channel_id=1, source_target_pairs={{0,2},{1,3},{2,0},{3,1},{4,6},{5,7},{6,4},{7,5},{8,10},{9,11},{10,... | collective-permute-start | bytes 10412 | tf_op jit(solution)/shard_map/ppermute | solution.py:348
  7.7 23.8 %all-to-all-start = ((f32[64,1,384]{2,1,0:T(1,128)}), f32[64,1,384]{2,1,0:T(1,128)S(1)}, u32[]{:S(2)}, u32[]{:S(2)}) async-start(f32[64,1,384]{2,1,0:T(1,128)} %shard_map.95), calls=%async_computation | async-start | bytes 196608 | tf_op jit(solution)/shard_map/all_to_all | solution.py:365
  31.5 3.9 %collective-permute-start.1 = (f32[64,384]{1,0:T(8,128)S(1)}, f32[64,384]{1,0:T(8,128)S(1)}, u32[]{:S(2)}, u32[]{:S(2)}) collective-permute-start(f32[64,384]{1,0:T(8,128)S(1)} %bitcast.23), channel_id=1, source_target_pairs={{0,2},{1,3},{2,0},{3,1},{4,6},{5,7},{6,4},{7,5},{8,10},{9,11},{10,... | collective-permute-start | bytes 294920 | tf_op jit(solution)/shard_map/ppermute | solution.py:348
  31.9 3.5 %collective-permute-start = (f32[64,384]{1,0:T(8,128)S(1)}, f32[64,384]{1,0:T(8,128)S(1)}, u32[]{:S(2)}, u32[]{:S(2)}) collective-permute-start(f32[64,384]{1,0:T(8,128)S(1)} %bitcast.24), channel_id=1, source_target_pairs={{0,1},{1,0},{2,3},{3,2},{4,5},{5,4},{6,7},{7,6},{8,9},{9,8},{10,11... | collective-permute-start | bytes 294920 | tf_op jit(solution)/shard_map/ppermute | solution.py:348
  34.3 5.4 %collective-permute-start.2 = (f32[64,384]{1,0:T(8,128)S(1)}, f32[64,384]{1,0:T(8,128)S(1)}, u32[]{:S(2)}, u32[]{:S(2)}) collective-permute-start(f32[64,384]{1,0:T(8,128)S(1)} %bitcast.25), channel_id=1, source_target_pairs={{0,3},{1,2},{2,1},{3,0},{4,7},{5,6},{6,5},{7,4},{8,11},{9,10},{10,... | collective-permute-start | bytes 294920 | tf_op jit(solution)/shard_map/ppermute | solution.py:348
  65.2 11.4 %collective-permute-start.6 = (bf16[256,768]{1,0:T(8,128)(2,1)S(1)}, bf16[256,768]{1,0:T(8,128)(2,1)S(1)}, u32[]{:S(2)}, u32[]{:S(2)}) collective-permute-start(bf16[256,768]{1,0:T(8,128)(2,1)S(1)} %get-tuple-element.4), channel_id=1, source_target_pairs={{0,2},{1,3},{2,0},{3,1},{4,6},{5,7},{6,4},{7,5},{8,10},{9,11},{10,... | collective-permute-start | bytes 1179656 | tf_op jit(solution)/shard_map/ppermute | solution.py:348
  65.5 19.1 %all-to-all-start.1 = ((f32[256,1,128]{2,1,0:T(1,128)}), f32[256,1,128]{2,1,0:T(1,128)S(1)}, u32[]{:S(2)}, u32[]{:S(2)}) async-start(f32[256,1,128]{2,1,0:T(1,128)} %bitcast.9), calls=%async_computation.1 | async-start | bytes 262144 | tf_op jit(solution)/shard_map/all_to_all | solution.py:370
  71.7 13.7 %collective-permute-start.8 = (bf16[256,768]{1,0:T(8,128)(2,1)S(1)}, bf16[256,768]{1,0:T(8,128)(2,1)S(1)}, u32[]{:S(2)}, u32[]{:S(2)}) collective-permute-start(bf16[256,768]{1,0:T(8,128)(2,1)S(1)} %get-tuple-element.4), channel_id=1, source_target_pairs={{0,1},{1,0},{2,3},{3,2},{4,5},{5,4},{6,7},{7,6},{8,9},{9,8},{10,11... | collective-permute-start | bytes 1179656 | tf_op jit(solution)/shard_map/ppermute | solution.py:348
  76.5 8.9 %collective-permute-start.7 = (bf16[256,768]{1,0:T(8,128)(2,1)S(1)}, bf16[256,768]{1,0:T(8,128)(2,1)S(1)}, u32[]{:S(2)}, u32[]{:S(2)}) collective-permute-start(bf16[256,768]{1,0:T(8,128)(2,1)S(1)} %collective-permute-done.6), channel_id=1, source_target_pairs={{0,1},{1,0},{2,3},{3,2},{4,5},{5,4},{6,7},{7,6},{8,9},{9,8},{10,11... | collective-permute-start | bytes 1179656 | tf_op jit(solution)/shard_map/ppermute | solution.py:348

commit v3 on v2

--- a/solution.py
+++ b/solution.py
@@ -20,6 +20,7 @@
 ROWS = 8
 MXU = 256
 PIECE = 16
+VMEM_LIMIT = 8 * 1024 * 1024
 BF = jnp.bfloat16
 F32 = jnp.float32
 
@@ -66,17 +67,18 @@
                 works.remove(work)
 
 
-def kernel(
-    points_ref, nodes_ref, recv_ref, offsets_ref,
-    trace_ref, image_ref,
-    field, recv, synth, band, gains, index, picture,
-    near0, near1, *push,
-):
-    slabs = points_ref.shape[0]
-    owners = points_ref.shape[1]
+def demigrate_kernel(first_slab, total, points_ref, nodes_ref, recv_ref, offsets_ref, *refs):
+    previous, refs = (refs[:3], refs[3:]) if first_slab else ((), refs)
+    last_call = first_slab + points_ref.shape[0] == total
+    (gains, index, synth), refs = refs[:3], refs[3:]
+    if last_call:
+        trace_ref, refs = refs[0], refs[1:]
+    field, recv, near0, near1, *push = refs
+    slabs, owners = points_ref.shape[:2]
     owned = points_ref.shape[2] // 4
     rows = owned // 2
     steps = rows // ROWS
+    row_base = first_slab * rows
     receivers = recv_ref.shape[1]
     part = PIECE
     pieces = BAND // part
@@ -84,7 +86,10 @@
 
     for k in range(3):
         recv[k] = jnp.broadcast_to(recv_ref[k], (receivers, LANES))
-    synth[...] = jnp.zeros_like(synth)
+    if previous:
+        synth[...] = previous[2][...]
+    else:
+        synth[...] = jnp.zeros_like(synth)
     for slab in range(slabs):
         turned = points_ref[slab].T
         for quantity in range(4):
@@ -107,9 +112,9 @@
         weight_even = jnp.where(is_odd, frac, 1.0 - frac)
         weight_odd = jnp.where(is_odd, 1.0 - frac, frac)
         for k, value in enumerate((even, lower, weight_even, weight_odd)):
-            index[k, octet(c), :] = value
-        x_near = (x - offsets_ref[slabs]) * (32.0 / NX)
-        y_near = (y - offsets_ref[slabs + 1]) * (32.0 / NX)
+            index[k, octet(row_base // ROWS + c), :] = value
+        x_near = (x - offsets_ref[total]) * (32.0 / NX)
+        y_near = (y - offsets_ref[total + 1]) * (32.0 / NX)
         square = x_near * x_near + y_near * y_near
         ready = (
             even, lower, amplitude * weight_even, amplitude * weight_odd, x_near, y_near, square
@@ -139,7 +144,7 @@
                     ],
                     axis=0,
                 ).astype(BF)
-                gains[c * ROWS + i, block : block + 16, :] = gain
+                gains[row_base + c * ROWS + i, block : block + 16, :] = gain
                 push[pair][k, block : block + 16, :] = gain
             yield
     def stack(pair, slot, sums):
@@ -149,14 +154,20 @@
             pair // 2, pair % 2, transpose=True,
         )
         wide = [
-            [jnp.broadcast_to(near[slot][k, i : i + 1, :], (16, LANES)).astype(BF) for i in group]
+            [jnp.broadcast_to(near[slot][k, i : i + 1, :], (8, LANES)) for i in group]
             for k in range(4)
         ]
         for tile in range(0, HALF, 16):
-            sample = (lax.broadcasted_iota(jnp.int32, (16, LANES), 0) + tile).astype(F32).astype(BF)
+            sample = lax.broadcasted_iota(jnp.int32, (8, LANES), 0).astype(F32)
             for half in range(2):
                 hat = [
-                    jnp.where(sample == wide[half][k], wide[2 + half][k], jnp.zeros((), BF))
+                    jnp.concatenate(
+                        [
+                            jnp.where(sample + float(tile + up) == wide[half][k], wide[2 + half][k], 0.0)
+                            for up in (0, 8)
+                        ],
+                        axis=0,
+                    ).astype(BF)
                     for k in range(2)
                 ]
                 pltpu.matmul_acc_lhs(
@@ -189,7 +200,7 @@
                 return 0
 
             lax.fori_loop(0, steps // 2, two, 0)
-            offset = offsets_ref[slab]
+            offset = offsets_ref[first_slab + slab]
             for k in range(pieces):
                 total = pltpu.matmul_pop(sums[0][k]) + pltpu.matmul_pop(sums[1][k])
                 half, start = divmod(k * part, HALF)
@@ -207,8 +218,23 @@
         *[pltpu.ACC(mxu_id=unit)((part, MXU), F32) for unit in range(2) for _ in range(pieces)],
     )
 
-    for col in range(0, receivers, LANES):
-        trace_ref[col : col + LANES, :] = synth[col // LANES, :SPAN, :].T.astype(BF)
+    if last_call:
+        for col in range(0, receivers, LANES):
+            trace_ref[col : col + LANES, :] = synth[col // LANES, :SPAN, :].T.astype(BF)
+
+
+def migrate_kernel(gains, index, synth, offsets_ref, image_ref, band, picture):
+    slabs = band.shape[0]
+    receivers = gains.shape[1]
+    rows = gains.shape[0] // slabs
+    owners = image_ref.shape[0] // slabs
+    steps = rows // ROWS
+    part = PIECE
+    pieces = BAND // part
+
+    def octet(c):
+        return pl.ds(pl.multiple_of(c * ROWS, ROWS), ROWS)
+
     for slab in range(slabs):
         offset = offsets_ref[slab]
         for half in range(2):
@@ -276,7 +302,8 @@
     for slab in range(slabs):
         whole = picture[slab * steps : (slab + 1) * steps].reshape(rows, LANES) * (1.0 / receivers)
         turned = jnp.concatenate([whole[:, :owners], whole[:, owners:]], axis=0).T
-        turned = jnp.concatenate([turned, jnp.zeros((owners, LANES - owned), F32)], axis=1)
+        blank = jnp.zeros((owners, LANES - turned.shape[1]), F32)
+        turned = jnp.concatenate([turned, blank], axis=1)
         image_ref[pl.ds(offsets_ref[slabs + 2 + slab], owners, stride=slabs), :] = turned
 
 
@@ -293,34 +320,56 @@
     out_ref[...] = jnp.broadcast_to(row[None], out_ref.shape)
 
 
-def probe(points, nodes, recv, offsets):
-    slabs, owners, width = points.shape
-    owned = width // 4
-    rows = owned // 2
-    receivers = recv.shape[1]
-    vmem = pl.BlockSpec(memory_space=pltpu.VMEM)
-    smem = pl.BlockSpec(memory_space=pltpu.SMEM)
+def call(kernel, outs, scratch, *args, aliases=None):
+    spaces = [pltpu.SMEM if arg.dtype == jnp.int32 else pltpu.VMEM for arg in args]
     return pl.pallas_call(
         kernel,
-        out_shape=[
-            jax.ShapeDtypeStruct((receivers, SPAN), BF),
-            jax.ShapeDtypeStruct((owners * slabs, LANES), F32),
-        ],
-        in_specs=[vmem, vmem, vmem, smem],
-        out_specs=[vmem, vmem],
-        scratch_shapes=[
+        out_shape=outs,
+        in_specs=[pl.BlockSpec(memory_space=space) for space in spaces],
+        out_specs=[pl.BlockSpec(memory_space=pltpu.VMEM) for _ in outs],
+        scratch_shapes=scratch,
+        input_output_aliases=aliases or {},
+        compiler_params=pltpu.CompilerParams(vmem_limit_bytes=VMEM_LIMIT),
+    )(*args)
+
+
+def demigrate_slabs(first_slab, total, points, nodes, recv, offsets, previous):
+    slabs, owners, width = points.shape
+    rows = width // 8
+    receivers = recv.shape[1]
+    outs = [
+        jax.ShapeDtypeStruct((total * rows, receivers, LANES), BF),
+        jax.ShapeDtypeStruct((4, total * rows, LANES), F32),
+        jax.ShapeDtypeStruct((receivers // LANES, NT, LANES), F32),
+    ]
+    if first_slab + slabs == total:
+        outs.append(jax.ShapeDtypeStruct((receivers, SPAN), BF))
+    return call(
+        functools.partial(demigrate_kernel, first_slab, total),
+        outs,
+        [
             pltpu.VMEM((4, slabs * rows, LANES), F32),
             pltpu.VMEM((3, receivers, LANES), F32),
-            pltpu.VMEM((receivers // LANES, NT, LANES), F32),
-            pltpu.VMEM((slabs, receivers // LANES, BAND, LANES), BF),
-            pltpu.VMEM((slabs * rows, receivers, LANES), BF),
-            pltpu.VMEM((4, slabs * rows, LANES), F32),
-            pltpu.VMEM((slabs * rows // ROWS, ROWS, LANES), F32),
             *[pltpu.VMEM((7, ROWS, LANES), F32) for _ in range(2)],
             *[pltpu.VMEM((2, receivers, LANES), BF) for _ in range(ROWS // 2)],
         ],
-        compiler_params=pltpu.CompilerParams(vmem_limit_bytes=48 * 1024 * 1024),
-    )(points, nodes, recv, offsets)
+        points, nodes, recv, offsets, *previous,
+        aliases={4 + k: k for k in range(len(previous))},
+    )
+
+
+def migrate_slabs(slabs, owners, gains, index, synth, offsets):
+    receivers = gains.shape[1]
+    rows = gains.shape[0] // slabs
+    return call(
+        migrate_kernel,
+        [jax.ShapeDtypeStruct((owners * slabs, LANES), F32)],
+        [
+            pltpu.VMEM((slabs, receivers // LANES, BAND, LANES), BF),
+            pltpu.VMEM((slabs * rows // ROWS, ROWS, LANES), F32),
+        ],
+        gains, index, synth, offsets,
+    )[0]
 
 
 def body(
@@ -342,6 +391,7 @@
     local = pl.pallas_call(
         pack, out_shape=jax.ShapeDtypeStruct((owners, 1, 4 * owned), F32)
     )(amplitudes, depth_cells, lateral_cells, jitter)
+    local, tables = lax.optimization_barrier((local, tables))
     swaps = [[(i, i ^ b) for i in range(slabs)] for b in range(slabs)]
 
     def swap(array, b):
@@ -363,14 +413,17 @@
     recv = jnp.stack([1.0 + near[0] * near[0] + near[1] * near[1], 2.0 * near[0], 2.0 * near[1]])
 
     mine = lax.all_to_all(local, "shot", 0, 0)[:, 0]
-    points = jnp.stack([swap(mine, b) for b in range(slabs)])
-
-    trace, image = probe(points, nodes, recv[:, :, None], offsets)
-
-    spread = lax.all_to_all(image, ("shot", "slab"), 0, 0)
+    others = jnp.stack([swap(mine, b) for b in range(1, slabs)])
+
+    recv = recv[:, :, None]
+    kept = demigrate_slabs(0, slabs, mine[None], nodes[:1], recv, offsets, [])
+    *kept, trace = demigrate_slabs(1, slabs, others, nodes[1:], recv, offsets, kept)
+    image = migrate_slabs(slabs, owners, *kept, offsets)
 
     near_trace = swap(trace, 1)
     far_trace = swap(trace, 2)
+    near_trace, far_trace, image = lax.optimization_barrier((near_trace, far_trace, image))
+    spread = lax.all_to_all(image, ("shot", "slab"), 0, 0)
     last_trace = swap(far_trace, 1)
     odd, upper = me % 2 == 1, me >= 2
 
@@ -384,7 +437,8 @@
     synthetic = jnp.pad(
         jnp.stack([first, second, third, fourth]).astype(F32), ((0, 0), (0, 0), (0, NT - SPAN))
     )
-    return (synthetic, jnp.sum(spread, axis=0)[None, :owned])
+    spread, synthetic = lax.optimization_barrier((spread, synthetic))
+    return (synthetic, jnp.sum(spread[:, :owned], axis=0)[None])
 
 
 def solution(mesh):

time: 88.4 us -> 83.1 us (0.940)
  waiting for transfers between devices: 20.1 us -> 12.9 us
  starting transfers between devices: 30.6 us -> 31.7 us
  Pallas kernels: 26.8 us -> 27.8 us
    ppermute x9, waiting for transfers between devices: 6.97 us -> 0.13 us  [swap(): return array if b == 0 else lax.ppermute(array, 'slab', swaps[b])]
    ppermute x9, starting transfers between devices: 11.8 us -> 7.32 us  [swap(): return array if b == 0 else lax.ppermute(array, 'slab', swaps[b])]
    all_to_all x1, waiting for transfers between devices: 5.72 us -> 2.54 us  [body(): mine = lax.all_to_all(local, 'shot', 0, 0)[:, 0]]
    all_to_all x1, starting transfers between devices: 6.2 us -> 9.26 us  [body(): spread = lax.all_to_all(image, ('shot', 'slab'), 0, 0)]
    all_to_all x1, waiting for transfers between devices: 7.42 us -> 10.2 us  [body(): spread = lax.all_to_all(image, ('shot', 'slab'), 0, 0)]
    all_to_all x1, starting transfers between devices: 12.6 us -> 15.1 us  [body(): mine = lax.all_to_all(local, 'shot', 0, 0)[:, 0]]
    pallas_call x1 -> x3, Pallas kernels: 25.4 us -> 26.4 us  [call(): pl.pallas_call(kernel, out_shape=outs, in_specs=[pl.BlockSpec(memory_spac...]
  transfers between devices with their start and end apart: 11 -> 11, of which waited for: 4 -> 3; matrix products, arithmetic and copies ran while one was open for 7% -> 11% of each run, Pallas kernels for 2% -> 19%
where the time goes in v3:
time: 83.1 us; the launch traced here: 82.8 us
  starting transfers between devices  31.7 us (38%)
  Pallas kernels  27.8 us (33%)
  waiting for transfers between devices  12.9 us (16%)
  local copies, waits for them, and re-layouts  5.56 us (7%)
  other arithmetic  4.01 us (5%)
    pallas_call x3, Pallas kernels, call(): pl.pallas_call(kernel, out_shape=outs, in_specs=[pl.BlockSpec(memory_spac...  26.4 us
    all_to_all x1, starting transfers between devices, body(): mine = lax.all_to_all(local, 'shot', 0, 0)[:, 0]  15.1 us
    all_to_all x1, waiting for transfers between devices, body(): spread = lax.all_to_all(image, ('shot', 'slab'), 0, 0)  10.2 us
    all_to_all x1, starting transfers between devices, body(): spread = lax.all_to_all(image, ('shot', 'slab'), 0, 0)  9.26 us
    ppermute x9, starting transfers between devices, swap(): return array if b == 0 else lax.ppermute(array, 'slab', swaps[b])  7.32 us
    concatenate x1, local copies, waits for them, and re-layouts, body(): jnp.concatenate([jnp.stack([pick(band_offsets, b) for b in range(slabs)])...  2.58 us
    pad x1, other arithmetic, body(): jnp.pad(jnp.stack([first, second, third, fourth]).astype(F32), ((0, 0), (...  2.58 us
    all_to_all x1, waiting for transfers between devices, body(): mine = lax.all_to_all(local, 'shot', 0, 0)[:, 0]  2.54 us
  transfers between devices with their start and end apart: 11, of which 3 were waited for; matrix products, arithmetic and copies ran while one was open for 11% of the time, Pallas kernels for 19%

profile of v3, /device:TPU:1, one launch (start us, length us, event | category | flops | bytes accessed | tf_op | source)
XLA Modules:
  0.0 82.8 jit_solution(8517982035827815790)
XLA Ops:
  0.6 0.0 copy-start
  0.6 1.5 %shard_map.95 = f32[64,1,384]{2,1,0:T(1,128)} custom-call(f32[1,96]{1,0:T(1,128)} %amplitudes_ref.1, s32[1,96]{1,0:T(1,128)} %depth_ref.1, s32[2,1,96]{2,1,0:T(1,128)} %lateral_ref.1, f32[3,1,96]{2,1,0:T(1,128)} %jitter_ref.1), custom_call_target="tpu_custom_call" | custom-call | tf_op jit(solution)/shard_map/pallas_call | solution.py:391
  2.1 15.1 %all-to-all-start = ((f32[64,1,384]{2,1,0:T(1,128)}), f32[64,1,384]{2,1,0:T(1,128)S(1)}, u32[]{:S(2)}, u32[]{:S(2)}) async-start(f32[64,1,384]{2,1,0:T(1,128)} %shard_map.95), calls=%async_computation | async-start | bytes 196608 | tf_op jit(solution)/shard_map/all_to_all | solution.py:415
  17.3 0.8 dynamic-slice_reduce_fusion.3
  18.0 1.2 %collective-permute-start.5 = (f32[867]{0:T(1024)S(1)}, f32[867]{0:T(1024)S(1)}, u32[]{:S(2)}, u32[]{:S(2)}) collective-permute-start(f32[867]{0:T(1024)S(1)} %get-tuple-element.31), channel_id=1, source_target_pairs={{0,3},{1,2},{2,1},{3,0},{4,7},{5,6},{6,5},{7,4},{8,11},{9,10},{10,... | collective-permute-start | bytes 10412 | tf_op jit(solution)/shard_map/ppermute | solution.py:398
  19.3 1.2 %collective-permute-start.4 = (f32[867]{0:T(1024)S(1)}, f32[867]{0:T(1024)S(1)}, u32[]{:S(2)}, u32[]{:S(2)}) collective-permute-start(f32[867]{0:T(1024)S(1)} %get-tuple-element.32), channel_id=1, source_target_pairs={{0,2},{1,3},{2,0},{3,1},{4,6},{5,7},{6,4},{7,5},{8,10},{9,11},{10,... | collective-permute-start | bytes 10412 | tf_op jit(solution)/shard_map/ppermute | solution.py:398
  20.4 0.0 collective-permute-start.3
  20.4 0.7 convert_multiply_fusion
  21.2 0.2 fusion.8
  21.4 0.1 stack.56
  21.4 0.2 copy.18.recv_ref
  21.6 1.5 %fusion.9 = (s32[1]{0:T(128)}, s32[1]{0:T(128)}, s32[1]{0:T(128)}, s32[1]{0:T(128)}) fusion(s32[4]{0:T(128)} %param.15, s32[]{:T(128)S(6)} %select_n.68, s32[]{:T(128)S(6)} %select_n.66, s32[]{:T(128)S(6)} %select_n.65, s32[]{:T(128)S(6)} %select_n.67), kind=kLoop, calls=%fused_computation.37 | loop fusion | bytes 48 | tf_op jit(solution)/shard_map/jit(dynamic_index_in_dim)/dynamic_slice | solution.py:401
  23.1 2.6 %concatenate.4.offsets_ref = s32[10]{0:T(128)S(1)} concatenate(s32[1]{0:T(128)} %get-tuple-element.45, s32[1]{0:T(128)} %get-tuple-element.44, s32[1]{0:T(128)} %get-tuple-element.46, s32[1]{0:T(128)} %get-tuple-element.43, s32[2]{0:T(128)S(1)} %fusion.8, s32[4]{0:T(128)S(1)} %iota_xor_fusion), dimensions={0} | concatenate | bytes 80 | tf_op jit(solution)/shard_map/concatenate | solution.py:409
  25.7 0.0 collective-permute-done.5
  25.7 0.1 stack.59
  25.8 0.1 stack.58
  25.8 0.1 stack.57
  25.9 2.5 %all-to-all-done = f32[64,1,384]{2,1,0:T(1,128)S(1)} async-done(((f32[64,1,384]{2,1,0:T(1,128)}), f32[64,1,384]{2,1,0:T(1,128)S(1)}, u32[]{:S(2)}, u32[]{:S(2)}) %all-to-all-start) | async-done | bytes 98336 | tf_op jit(solution)/shard_map/all_to_all | solution.py:415
  28.5 0.4 collective-permute-start.1
  28.9 2.4 %collective-permute-start = (f32[64,384]{1,0:T(8,128)S(1)}, f32[64,384]{1,0:T(8,128)S(1)}, u32[]{:S(2)}, u32[]{:S(2)}) collective-permute-start(f32[64,384]{1,0:T(8,128)S(1)} %bitcast.24), channel_id=1, source_target_pairs={{0,1},{1,0},{2,3},{3,2},{4,5},{5,4},{6,7},{7,6},{8,9},{9,8},{10,11... | collective-permute-start | bytes 294920 | tf_op jit(solution)/shard_map/ppermute | solution.py:398
  31.3 1.0 %collective-permute-start.2 = (f32[64,384]{1,0:T(8,128)S(1)}, f32[64,384]{1,0:T(8,128)S(1)}, u32[]{:S(2)}, u32[]{:S(2)}) collective-permute-start(f32[64,384]{1,0:T(8,128)S(1)} %bitcast.25), channel_id=1, source_target_pairs={{0,3},{1,2},{2,1},{3,0},{4,7},{5,6},{6,5},{7,4},{8,11},{9,10},{10,... | collective-permute-start | bytes 294920 | tf_op jit(solution)/shard_map/ppermute | solution.py:398
  32.4 4.2 %shard_map.96 = (bf16[192,256,128]{2,1,0:T(8,128)(2,1)S(1)}, f32[4,192,128]{2,1,0:T(8,128)S(1)}, f32[2,1024,128]{2,1,0:T(8,128)S(1)}) custom-call(f32[1,64,384]{2,1,0:T(8,128)S(1)} %bitcast.26, f32[1,9,128]{2,1,0:T(8,128)S(1)} %slice.30.nodes_ref, f32[3,256,1]{2,1,0:T(8,128)S(1)} %copy.18.recv_ref, s32[10]{0:T(128)S(1)} %concatenate.4.offsets_ref), custom_call_target="tpu_custom_call" | custom-call | tf_op jit(solution)/shard_map/pallas_call | solution.py:325
  36.6 0.1 collective-permute-done.2
  36.7 10.6 %shard_map.97 = (bf16[192,256,128]{2,1,0:T(8,128)(2,1)S(1)}, f32[4,192,128]{2,1,0:T(8,128)S(1)}, f32[2,1024,128]{2,1,0:T(8,128)S(1)}, bf16[256,768]{1,0:T(8,128)(2,1)S(1)}) custom-call(f32[3,64,384]{2,1,0:T(8,128)S(1)} %pad_maximum_fusion.points_ref, f32[3,9,128]{2,1,0:T(8,128)S(1)} %slice.26.nodes_ref, ...), custom_call_target="tpu_custom_call", output_to_operand_aliasing={{0}: (4, {}), {1}: (5, {}), {2}: (6, {})} | custom-call | tf_op jit(solution)/shard_map/pallas_call | solution.py:325
  47.3 0.4 collective-permute-start.7
  47.7 0.7 collective-permute-start.6
  48.4 11.6 %shard_map.98 = f32[256,128]{1,0:T(8,128)} custom-call(bf16[192,256,128]{2,1,0:T(8,128)(2,1)S(1)} %get-tuple-element.22.gains, f32[4,192,128]{2,1,0:T(8,128)S(1)} %get-tuple-element.23.index, f32[2,1024,128]{2,1,0:T(8,128)S(1)} %get-tuple-element.24.synth, s32[10]{0:T(128)S(1)} %concatenate.4.offsets_ref), custom_call_target="tpu_custom_call" | custom-call | tf_op jit(solution)/shard_map/pallas_call | solution.py:325
  60.0 9.3 %all-to-all-start.1 = ((f32[256,1,128]{2,1,0:T(1,128)}), f32[256,1,128]{2,1,0:T(1,128)S(1)}, u32[]{:S(2)}, u32[]{:S(2)}) async-start(f32[256,1,128]{2,1,0:T(1,128)} %bitcast.5), calls=%async_computation.1 | async-start | bytes 262144 | tf_op jit(solution)/shard_map/all_to_all | solution.py:426
  69.3 0.1 select_bitcast_fusion.3
  69.4 2.6 %fusion.7 = f32[4,256,1024]{2,1,0:T(8,128)} fusion(bf16[1,256,768]{2,1,0:T(8,128)(2,1)S(1)} %get-tuple-element.37, bf16[1,256,768]{2,1,0:T(8,128)(2,1)S(1)} %get-tuple-element.36, bf16[1,256,768]{2,1,0:T(8,128)(2,1)S(1)} %get-tuple-element.35, bf16[1,256,768]{2,1,0:T(8,128)(2,1)S(1)} %get-tuple-element.34), kind=kLoop, calls=%fused_computation.8 | loop fusion | flops 13631488 | bytes 5767168 | tf_op jit(solution)/shard_map/jit(_pad)/pad | solution.py:437
  72.0 10.2 %all-to-all-done.1 = f32[256,1,128]{2,1,0:T(1,128)S(1)} async-done(((f32[256,1,128]{2,1,0:T(1,128)}), f32[256,1,128]{2,1,0:T(1,128)S(1)}, u32[]{:S(2)}, u32[]{:S(2)}) %all-to-all-start.1) | async-done | bytes 131104 | tf_op jit(solution)/shard_map/all_to_all | solution.py:426
  82.3 0.6 slice_reduce_fusion
  (19 shorter events, 0.1 us)
Async XLA Ops:
  0.6 20.5 %copy-start = (s32[2,4]{1,0:T(2,128)S(1)}, s32[2,4]{1,0:T(2,128)}, u32[]{:S(2)}) copy-start(s32[2,4]{1,0:T(2,128)} %param.13) | copy-start | bytes 100
  2.1 26.3 %all-to-all-start = ((f32[64,1,384]{2,1,0:T(1,128)}), f32[64,1,384]{2,1,0:T(1,128)S(1)}, u32[]{:S(2)}, u32[]{:S(2)}) async-start(f32[64,1,384]{2,1,0:T(1,128)} %shard_map.95), calls=%async_computation | async-start | bytes 196608 | tf_op jit(solution)/shard_map/all_to_all | solution.py:415
  18.0 7.6 %collective-permute-start.5 = (f32[867]{0:T(1024)S(1)}, f32[867]{0:T(1024)S(1)}, u32[]{:S(2)}, u32[]{:S(2)}) collective-permute-start(f32[867]{0:T(1024)S(1)} %get-tuple-element.31), channel_id=1, source_target_pairs={{0,3},{1,2},{2,1},{3,0},{4,7},{5,6},{6,5},{7,4},{8,11},{9,10},{10,... | collective-permute-start | bytes 10412 | tf_op jit(solution)/shard_map/ppermute | solution.py:398
  19.3 6.5 %collective-permute-start.4 = (f32[867]{0:T(1024)S(1)}, f32[867]{0:T(1024)S(1)}, u32[]{:S(2)}, u32[]{:S(2)}) collective-permute-start(f32[867]{0:T(1024)S(1)} %get-tuple-element.32), channel_id=1, source_target_pairs={{0,2},{1,3},{2,0},{3,1},{4,6},{5,7},{6,4},{7,5},{8,10},{9,11},{10,... | collective-permute-start | bytes 10412 | tf_op jit(solution)/shard_map/ppermute | solution.py:398
  20.4 5.4 %collective-permute-start.3 = (f32[867]{0:T(1024)S(1)}, f32[867]{0:T(1024)S(1)}, u32[]{:S(2)}, u32[]{:S(2)}) collective-permute-start(f32[867]{0:T(1024)S(1)} %get-tuple-element.33), channel_id=1, source_target_pairs={{0,1},{1,0},{2,3},{3,2},{4,5},{5,4},{6,7},{7,6},{8,9},{9,8},{10,11... | collective-permute-start | bytes 10412 | tf_op jit(solution)/shard_map/ppermute | solution.py:398
  28.5 8.1 %collective-permute-start.1 = (f32[64,384]{1,0:T(8,128)S(1)}, f32[64,384]{1,0:T(8,128)S(1)}, u32[]{:S(2)}, u32[]{:S(2)}) collective-permute-start(f32[64,384]{1,0:T(8,128)S(1)} %bitcast.23), channel_id=1, source_target_pairs={{0,2},{1,3},{2,0},{3,1},{4,6},{5,7},{6,4},{7,5},{8,10},{9,11},{10,... | collective-permute-start | bytes 294920 | tf_op jit(solution)/shard_map/ppermute | solution.py:398
  28.9 7.7 %collective-permute-start = (f32[64,384]{1,0:T(8,128)S(1)}, f32[64,384]{1,0:T(8,128)S(1)}, u32[]{:S(2)}, u32[]{:S(2)}) collective-permute-start(f32[64,384]{1,0:T(8,128)S(1)} %bitcast.24), channel_id=1, source_target_pairs={{0,1},{1,0},{2,3},{3,2},{4,5},{5,4},{6,7},{7,6},{8,9},{9,8},{10,11... | collective-permute-start | bytes 294920 | tf_op jit(solution)/shard_map/ppermute | solution.py:398
  31.3 5.4 %collective-permute-start.2 = (f32[64,384]{1,0:T(8,128)S(1)}, f32[64,384]{1,0:T(8,128)S(1)}, u32[]{:S(2)}, u32[]{:S(2)}) collective-permute-start(f32[64,384]{1,0:T(8,128)S(1)} %bitcast.25), channel_id=1, source_target_pairs={{0,3},{1,2},{2,1},{3,0},{4,7},{5,6},{6,5},{7,4},{8,11},{9,10},{10,... | collective-permute-start | bytes 294920 | tf_op jit(solution)/shard_map/ppermute | solution.py:398
  47.3 12.7 %collective-permute-start.7 = (bf16[256,768]{1,0:T(8,128)(2,1)S(1)}, bf16[256,768]{1,0:T(8,128)(2,1)S(1)}, u32[]{:S(2)}, u32[]{:S(2)}) collective-permute-start(bf16[256,768]{1,0:T(8,128)(2,1)S(1)} %get-tuple-element.21), channel_id=1, source_target_pairs={{0,2},{1,3},{2,0},{3,1},{4,6},{5,7},{6,4},{7,5},{8,10},{9,11},{10,... | collective-permute-start | bytes 1179656 | tf_op jit(solution)/shard_map/ppermute | solution.py:398
  47.7 12.3 %collective-permute-start.6 = (bf16[256,768]{1,0:T(8,128)(2,1)S(1)}, bf16[256,768]{1,0:T(8,128)(2,1)S(1)}, u32[]{:S(2)}, u32[]{:S(2)}) collective-permute-start(bf16[256,768]{1,0:T(8,128)(2,1)S(1)} %get-tuple-element.21), channel_id=1, source_target_pairs={{0,1},{1,0},{2,3},{3,2},{4,5},{5,4},{6,7},{7,6},{8,9},{9,8},{10,11... | collective-permute-start | bytes 1179656 | tf_op jit(solution)/shard_map/ppermute | solution.py:398
  60.0 9.3 %collective-permute-start.8 = (bf16[256,768]{1,0:T(8,128)(2,1)S(1)}, bf16[256,768]{1,0:T(8,128)(2,1)S(1)}, u32[]{:S(2)}, u32[]{:S(2)}) collective-permute-start(bf16[256,768]{1,0:T(8,128)(2,1)S(1)} %collective-permute-done.7), channel_id=1, source_target_pairs={{0,1},{1,0},{2,3},{3,2},{4,5},{5,4},{6,7},{7,6},{8,9},{9,8},{10,11... | collective-permute-start | bytes 1179656 | tf_op jit(solution)/shard_map/ppermute | solution.py:398
  60.0 22.2 %all-to-all-start.1 = ((f32[256,1,128]{2,1,0:T(1,128)}), f32[256,1,128]{2,1,0:T(1,128)S(1)}, u32[]{:S(2)}, u32[]{:S(2)}) async-start(f32[256,1,128]{2,1,0:T(1,128)} %bitcast.5), calls=%async_computation.1 | async-start | bytes 262144 | tf_op jit(solution)/shard_map/all_to_all | solution.py:426

commit v4 on v3

--- a/solution.py
+++ b/solution.py
@@ -16,46 +16,42 @@
 ND = 3
 SPAN = 768
 LANES = 128
-SEGMENTS = 3
 ROWS = 8
 MXU = 256
 PIECE = 16
+MIG_SPAN = 6
 VMEM_LIMIT = 8 * 1024 * 1024
 BF = jnp.bfloat16
 F32 = jnp.float32
 
 
 def travel_octet(z, x, y, table):
-    x_scaled = x / SPACING
     z_scaled = z / SPACING
-    y_scaled = y / SPACING
-    x_cell = jnp.floor(x_scaled)
-    y_cell = jnp.floor(y_scaled)
-    x_part = x_scaled - x_cell
-    y_part = y_scaled - y_cell
-    node = (x_cell * NL + y_cell).astype(jnp.int32)
+    parts, cells = [], []
+    for scaled in (x / SPACING, y / SPACING):
+        cell = jnp.minimum(jnp.floor(scaled), float(NL - 2))
+        cells.append(cell)
+        parts.append(scaled - cell)
+    at = (cells[0] * (NL - 1) + cells[1]).astype(jnp.int32)
+    lane = at & (LANES - 1)
+    lower = at < LANES
     total = jnp.zeros_like(z)
-    corner_weights = ((1.0 - x_part, x_part), (1.0 - y_part, y_part))
+    sides = [(1.0 - part, part) for part in parts]
     plane_weights = [jnp.maximum(0.0, 1.0 - jnp.abs(z_scaled - float(a))) for a in range(ND)]
-    for b in range(2):
-        for c in range(2):
-            at = node + (b * NL + c)
-            lane = at & (LANES - 1)
-            block = at >> 7
-            first, second = block == 0, block == 1
-            value = jnp.zeros_like(z)
-            for a in range(ND):
-                found = [
-                    jnp.take_along_axis(
-                        jnp.broadcast_to(table[SEGMENTS * a + k : SEGMENTS * a + k + 1], z.shape),
-                        lane, axis=1, mode="promise_in_bounds",
-                    )
-                    for k in range(SEGMENTS)
-                ]
-                picked = jnp.where(first, found[0], jnp.where(second, found[1], found[2]))
-                value = value + plane_weights[a] * picked
-                yield
-            total = total + (corner_weights[0][b] * corner_weights[1][c]) * value
+    for corner in range(4):
+        value = jnp.zeros_like(z)
+        for a in range(ND):
+            row = 2 * (ND * corner + a)
+            found = [
+                jnp.take_along_axis(
+                    jnp.broadcast_to(table[row + k : row + k + 1], z.shape),
+                    lane, axis=1, mode="promise_in_bounds",
+                )
+                for k in range(2)
+            ]
+            value = value + plane_weights[a] * jnp.where(lower, found[0], found[1])
+            yield
+        total = total + (sides[0][corner // 2] * sides[1][corner % 2]) * value
     return total
 
 
@@ -193,13 +189,14 @@
             )
 
         def one_slab(slab, _):
-            def two(j, _):
-                c = slab * steps + 2 * j
-                phase(c, 0)
-                phase(c + 1, 1)
+            span = 2 if slabs == 1 else steps
+
+            def several(j, _):
+                for k in range(span):
+                    phase(slab * steps + j * span + k, k % 2)
                 return 0
 
-            lax.fori_loop(0, steps // 2, two, 0)
+            lax.fori_loop(0, steps // span, several, 0)
             offset = offsets_ref[first_slab + slab]
             for k in range(pieces):
                 total = pltpu.matmul_pop(sums[0][k]) + pltpu.matmul_pop(sums[1][k])
@@ -285,15 +282,17 @@
 
         count = slabs * steps
 
-        def step(c, _):
-            interleave(correlate(c, 0), correlate(c, 1), collect(c - 1, 2), collect(c - 1, 3))
-            interleave(correlate(c, 2), correlate(c, 3), collect(c, 0), collect(c, 1))
+        def octets(j, _):
+            for k in range(MIG_SPAN):
+                c = MIG_SPAN * j + k
+                interleave(correlate(c, 2), correlate(c, 3), collect(c, 0), collect(c, 1))
+                ahead = jnp.minimum(c + 1, count - 1)
+                interleave(correlate(ahead, 0), correlate(ahead, 1), collect(c, 2), collect(c, 3))
             return 0
 
         interleave(correlate(0, 0), correlate(0, 1))
-        interleave(correlate(0, 2), correlate(0, 3), collect(0, 0), collect(0, 1))
-        lax.fori_loop(1, count, step, 0)
-        interleave(collect(count - 1, 2), collect(count - 1, 3))
+        lax.fori_loop(0, count // MIG_SPAN, octets, 0)
+        interleave(collect(count - 1, 0), collect(count - 1, 1))
 
     pl.run_scoped(
         migrate,
@@ -338,9 +337,9 @@
     rows = width // 8
     receivers = recv.shape[1]
     outs = [
-        jax.ShapeDtypeStruct((total * rows, receivers, LANES), BF),
-        jax.ShapeDtypeStruct((4, total * rows, LANES), F32),
-        jax.ShapeDtypeStruct((receivers // LANES, NT, LANES), F32),
+        pltpu.VMEM((total * rows, receivers, LANES), BF),
+        pltpu.VMEM((4, total * rows, LANES), F32),
+        pltpu.VMEM((receivers // LANES, NT, LANES), F32),
     ]
     if first_slab + slabs == total:
         outs.append(jax.ShapeDtypeStruct((receivers, SPAN), BF))
@@ -401,9 +400,13 @@
         return lax.dynamic_index_in_dim(array, me ^ b, axis, keepdims=False)
 
     table = jnp.stack([swap(pick(tables[:, 0, :], b), b) for b in range(slabs)])
-    nodes = jnp.pad(
-        table.reshape(slabs, ND, NL * NL), ((0, 0), (0, 0), (0, SEGMENTS * LANES - NL * NL))
-    ).reshape(slabs, ND * SEGMENTS, LANES)
+    table = table.reshape(slabs, ND, NL, NL)
+    corners = [
+        table[:, :, b : b + NL - 1, c : c + NL - 1].reshape(slabs, 2 * ND, LANES)
+        for b in range(2)
+        for c in range(2)
+    ]
+    nodes = jnp.concatenate(corners, axis=1)
     shot = pick(shot_cells, 0, 1)
     places = me ^ jnp.arange(slabs, dtype=jnp.int32)
     offsets = jnp.concatenate(
@@ -422,8 +425,8 @@
 
     near_trace = swap(trace, 1)
     far_trace = swap(trace, 2)
-    near_trace, far_trace, image = lax.optimization_barrier((near_trace, far_trace, image))
     spread = lax.all_to_all(image, ("shot", "slab"), 0, 0)
+    near_trace, far_trace, _ = lax.optimization_barrier((near_trace, far_trace, image))
     last_trace = swap(far_trace, 1)
     odd, upper = me % 2 == 1, me >= 2
 

time: 83.1 us -> 80.6 us (0.970)
  Pallas kernels: 27.8 us -> 24 us
    pallas_call x3, Pallas kernels: 26.4 us -> 22.6 us  [call(): pl.pallas_call(kernel, out_shape=outs, in_specs=[pl.BlockSpec(memory_spac...]
    ppermute x9, starting transfers between devices: 7.32 us -> 8.3 us  [swap(): return array if b == 0 else lax.ppermute(array, 'slab', swaps[b])]
  transfers between devices with their start and end apart: 11 -> 11, of which waited for: 3 -> 4; matrix products, arithmetic and copies ran while one was open for 11% -> 12% of each run, Pallas kernels for 19% -> 16%
where the time goes in v4:
time: 80.6 us; the launch traced here: 80.3 us
  starting transfers between devices  32.4 us (40%)
  Pallas kernels  24 us (30%)
  waiting for transfers between devices  12.9 us (16%)
  local copies, waits for them, and re-layouts  6.08 us (8%)
  other arithmetic  4.03 us (5%)
  between operations  0.86 us (1%)
    pallas_call x3, Pallas kernels, call(): pl.pallas_call(kernel, out_shape=outs, in_specs=[pl.BlockSpec(memory_spac...  22.6 us
    all_to_all x1, starting transfers between devices, body(): mine = lax.all_to_all(local, 'shot', 0, 0)[:, 0]  15.1 us
    all_to_all x1, waiting for transfers between devices, body(): spread = lax.all_to_all(image, ('shot', 'slab'), 0, 0)  10.2 us
    all_to_all x1, starting transfers between devices, body(): spread = lax.all_to_all(image, ('shot', 'slab'), 0, 0)  9.02 us
    ppermute x9, starting transfers between devices, swap(): return array if b == 0 else lax.ppermute(array, 'slab', swaps[b])  8.3 us
    pad x1, other arithmetic, body(): jnp.pad(jnp.stack([first, second, third, fourth]).astype(F32), ((0, 0), (...  2.58 us
    concatenate x1, local copies, waits for them, and re-layouts, body(): jnp.concatenate([jnp.stack([pick(band_offsets, b) for b in range(slabs)])...  2.51 us
    dynamic_slice x3, local copies, waits for them, and re-layouts, pick(): return lax.dynamic_index_in_dim(array, me ^ b, axis, keepdims=False)  2.4 us
  transfers between devices with their start and end apart: 11, of which 4 were waited for; matrix products, arithmetic and copies ran while one was open for 12% of the time, Pallas kernels for 16%

profile of v4, /device:TPU:1, one launch (start us, length us, event | category | flops | bytes accessed | tf_op | source)
XLA Modules:
  0.0 80.3 jit_solution(6493466347207794748)
XLA Ops:
  0.6 1.5 %shard_map.95 = f32[64,1,384]{2,1,0:T(1,128)} custom-call(f32[1,96]{1,0:T(1,128)} %amplitudes_ref.1, s32[1,96]{1,0:T(1,128)} %depth_ref.1, s32[2,1,96]{2,1,0:T(1,128)} %lateral_ref.1, f32[3,1,96]{2,1,0:T(1,128)} %jitter_ref.1), custom_call_target="tpu_custom_call" | custom-call | tf_op jit(solution)/shard_map/pallas_call | solution.py:390
  2.1 15.1 %all-to-all-start = ((f32[64,1,384]{2,1,0:T(1,128)}), f32[64,1,384]{2,1,0:T(1,128)S(1)}, u32[]{:S(2)}, u32[]{:S(2)}) async-start(f32[64,1,384]{2,1,0:T(1,128)} %shard_map.95), calls=%async_computation | async-start | bytes 196608 | tf_op jit(solution)/shard_map/all_to_all | solution.py:418
  17.3 0.8 dynamic-slice_reduce_fusion
  18.0 1.2 %collective-permute-start.5 = (f32[867]{0:T(1024)S(1)}, f32[867]{0:T(1024)S(1)}, u32[]{:S(2)}, u32[]{:S(2)}) collective-permute-start(f32[867]{0:T(1024)S(1)} %get-tuple-element.28), channel_id=1, source_target_pairs={{0,3},{1,2},{2,1},{3,0},{4,7},{5,6},{6,5},{7,4},{8,11},{9,10},{10,... | collective-permute-start | bytes 10412 | tf_op jit(solution)/shard_map/ppermute | solution.py:397
  19.3 1.2 %collective-permute-start.4 = (f32[867]{0:T(1024)S(1)}, f32[867]{0:T(1024)S(1)}, u32[]{:S(2)}, u32[]{:S(2)}) collective-permute-start(f32[867]{0:T(1024)S(1)} %get-tuple-element.29), channel_id=1, source_target_pairs={{0,2},{1,3},{2,0},{3,1},{4,6},{5,7},{6,4},{7,5},{8,10},{9,11},{10,... | collective-permute-start | bytes 10412 | tf_op jit(solution)/shard_map/ppermute | solution.py:397
  20.4 0.7 convert_multiply_fusion
  21.1 0.1 stack.56
  21.3 0.2 fusion.8
  21.5 0.2 copy.18.recv_ref
  21.7 1.4 %fusion.10 = (s32[1]{0:T(128)}, s32[1]{0:T(128)}, s32[1]{0:T(128)}, s32[1]{0:T(128)}) fusion(s32[4]{0:T(128)} %param.15, s32[]{:T(128)S(6)} %select_n.68, s32[]{:T(128)S(6)} %select_n.66, s32[]{:T(128)S(6)} %select_n.65, s32[]{:T(128)S(6)} %select_n.67), kind=kLoop, calls=%fused_computation.40 | loop fusion | bytes 48 | tf_op jit(solution)/shard_map/jit(dynamic_index_in_dim)/dynamic_slice | solution.py:400
  23.1 2.5 %concatenate.8.offsets_ref = s32[10]{0:T(128)S(1)} concatenate(s32[1]{0:T(128)} %get-tuple-element.47, s32[1]{0:T(128)} %get-tuple-element.46, s32[1]{0:T(128)} %get-tuple-element.48, s32[1]{0:T(128)} %get-tuple-element.45, s32[2]{0:T(128)S(1)} %fusion.8, s32[4]{0:T(128)S(1)} %iota_xor_fusion), dimensions={0} | concatenate | bytes 80 | tf_op jit(solution)/shard_map/concatenate | solution.py:412
  25.6 0.1 stack.57
  25.8 0.1 stack.58
  25.9 0.1 stack.59
  26.0 0.1 fusion.9
  26.6 1.9 %all-to-all-done = f32[64,1,384]{2,1,0:T(1,128)S(1)} async-done(((f32[64,1,384]{2,1,0:T(1,128)}), f32[64,1,384]{2,1,0:T(1,128)S(1)}, u32[]{:S(2)}, u32[]{:S(2)}) %all-to-all-start) | async-done | bytes 98336 | tf_op jit(solution)/shard_map/all_to_all | solution.py:418
  28.5 0.4 collective-permute-start.1
  28.9 2.4 %collective-permute-start = (f32[64,384]{1,0:T(8,128)S(1)}, f32[64,384]{1,0:T(8,128)S(1)}, u32[]{:S(2)}, u32[]{:S(2)}) collective-permute-start(f32[64,384]{1,0:T(8,128)S(1)} %bitcast.32), channel_id=1, source_target_pairs={{0,1},{1,0},{2,3},{3,2},{4,5},{5,4},{6,7},{7,6},{8,9},{9,8},{10,11... | collective-permute-start | bytes 294920 | tf_op jit(solution)/shard_map/ppermute | solution.py:397
  31.3 1.0 %collective-permute-start.2 = (f32[64,384]{1,0:T(8,128)S(1)}, f32[64,384]{1,0:T(8,128)S(1)}, u32[]{:S(2)}, u32[]{:S(2)}) collective-permute-start(f32[64,384]{1,0:T(8,128)S(1)} %bitcast.33), channel_id=1, source_target_pairs={{0,3},{1,2},{2,1},{3,0},{4,7},{5,6},{6,5},{7,4},{8,11},{9,10},{10,... | collective-permute-start | bytes 294920 | tf_op jit(solution)/shard_map/ppermute | solution.py:397
  32.3 4.1 %shard_map.96 = (bf16[192,256,128]{2,1,0:T(8,128)(2,1)S(1)}, f32[4,192,128]{2,1,0:T(8,128)S(1)}, f32[2,1024,128]{2,1,0:T(8,128)S(1)}) custom-call(f32[1,64,384]{2,1,0:T(8,128)S(1)} %bitcast.34, f32[1,24,128]{2,1,0:T(8,128)S(1)} %pad_maximum_fusion.2.nodes_ref, f32[3,256,1]{2,1,0:T(8,128)S(1)} %copy.18.recv_ref, s32[10]{0:T(128)S(1)} %concatenate.8.offsets_ref), custom_call_target="tpu_custom_call" | custom-call | tf_op jit(solution)/shard_map/pallas_call | solution.py:324
  36.5 0.2 collective-permute-done.2
  36.7 9.4 %shard_map.97 = (bf16[192,256,128]{2,1,0:T(8,128)(2,1)S(1)}, f32[4,192,128]{2,1,0:T(8,128)S(1)}, f32[2,1024,128]{2,1,0:T(8,128)S(1)}, bf16[256,768]{1,0:T(8,128)(2,1)S(1)}) custom-call(f32[3,64,384]{2,1,0:T(8,128)S(1)} %pad_maximum_fusion.points_ref, f32[3,24,128]{2,1,0:T(8,128)S(1)} %slice.44.nodes_ref, ...), custom_call_target="tpu_custom_call", output_to_operand_aliasing={{0}: (4, {}), {1}: (5, {}), {2}: (6, {})} | custom-call | tf_op jit(solution)/shard_map/pallas_call | solution.py:324
  46.2 0.4 collective-permute-start.7
  46.5 0.6 collective-permute-start.6
  47.1 9.0 %shard_map.98 = f32[256,128]{1,0:T(8,128)} custom-call(bf16[192,256,128]{2,1,0:T(8,128)(2,1)S(1)} %get-tuple-element.20.gains, f32[4,192,128]{2,1,0:T(8,128)S(1)} %get-tuple-element.21.index, f32[2,1024,128]{2,1,0:T(8,128)S(1)} %get-tuple-element.22.synth, s32[10]{0:T(128)S(1)} %concatenate.8.offsets_ref), custom_call_target="tpu_custom_call" | custom-call | tf_op jit(solution)/shard_map/pallas_call | solution.py:324
  56.1 0.5 collective-permute-done.7
  56.7 1.1 %collective-permute-start.8 = (bf16[256,768]{1,0:T(8,128)(2,1)S(1)}, bf16[256,768]{1,0:T(8,128)(2,1)S(1)}, u32[]{:S(2)}, u32[]{:S(2)}) collective-permute-start(bf16[256,768]{1,0:T(8,128)(2,1)S(1)} %collective-permute-done.7), channel_id=1, source_target_pairs={{0,1},{1,0},{2,3},{3,2},{4,5},{5,4},{6,7},{7,6},{8,9},{9,8},{10,11... | collective-permute-start | bytes 1179656 | tf_op jit(solution)/shard_map/ppermute | solution.py:397
  57.8 9.0 %all-to-all-start.1 = ((f32[256,1,128]{2,1,0:T(1,128)}), f32[256,1,128]{2,1,0:T(1,128)S(1)}, u32[]{:S(2)}, u32[]{:S(2)}) async-start(f32[256,1,128]{2,1,0:T(1,128)} %bitcast.5), calls=%async_computation.1 | async-start | bytes 262144 | tf_op jit(solution)/shard_map/all_to_all | solution.py:428
  66.8 0.1 select_bitcast_fusion.3
  67.0 2.6 %fusion.7 = f32[4,256,1024]{2,1,0:T(8,128)} fusion(bf16[1,256,768]{2,1,0:T(8,128)(2,1)S(1)} %get-tuple-element.35, bf16[1,256,768]{2,1,0:T(8,128)(2,1)S(1)} %get-tuple-element.34, bf16[1,256,768]{2,1,0:T(8,128)(2,1)S(1)} %get-tuple-element.33, bf16[1,256,768]{2,1,0:T(8,128)(2,1)S(1)} %get-tuple-element.32), kind=kLoop, calls=%fused_computation.8 | loop fusion | flops 13631488 | bytes 5767168 | tf_op jit(solution)/shard_map/jit(_pad)/pad | solution.py:440
  69.5 10.2 %all-to-all-done.1 = f32[256,1,128]{2,1,0:T(1,128)S(1)} async-done(((f32[256,1,128]{2,1,0:T(1,128)}), f32[256,1,128]{2,1,0:T(1,128)S(1)}, u32[]{:S(2)}, u32[]{:S(2)}) %all-to-all-start.1) | async-done | bytes 131104 | tf_op jit(solution)/shard_map/all_to_all | solution.py:428
  79.8 0.6 slice_reduce_fusion
  (26 shorter events, 0.5 us)
Async XLA Ops:
  0.6 20.7 %copy-start = (s32[2,4]{1,0:T(2,128)S(1)}, s32[2,4]{1,0:T(2,128)}, u32[]{:S(2)}) copy-start(s32[2,4]{1,0:T(2,128)} %param.13) | copy-start | bytes 100
  2.1 26.3 %all-to-all-start = ((f32[64,1,384]{2,1,0:T(1,128)}), f32[64,1,384]{2,1,0:T(1,128)S(1)}, u32[]{:S(2)}, u32[]{:S(2)}) async-start(f32[64,1,384]{2,1,0:T(1,128)} %shard_map.95), calls=%async_computation | async-start | bytes 196608 | tf_op jit(solution)/shard_map/all_to_all | solution.py:418
  18.0 7.9 %collective-permute-start.5 = (f32[867]{0:T(1024)S(1)}, f32[867]{0:T(1024)S(1)}, u32[]{:S(2)}, u32[]{:S(2)}) collective-permute-start(f32[867]{0:T(1024)S(1)} %get-tuple-element.28), channel_id=1, source_target_pairs={{0,3},{1,2},{2,1},{3,0},{4,7},{5,6},{6,5},{7,4},{8,11},{9,10},{10,... | collective-permute-start | bytes 10412 | tf_op jit(solution)/shard_map/ppermute | solution.py:397
  19.3 6.5 %collective-permute-start.4 = (f32[867]{0:T(1024)S(1)}, f32[867]{0:T(1024)S(1)}, u32[]{:S(2)}, u32[]{:S(2)}) collective-permute-start(f32[867]{0:T(1024)S(1)} %get-tuple-element.29), channel_id=1, source_target_pairs={{0,2},{1,3},{2,0},{3,1},{4,6},{5,7},{6,4},{7,5},{8,10},{9,11},{10,... | collective-permute-start | bytes 10412 | tf_op jit(solution)/shard_map/ppermute | solution.py:397
  20.4 5.2 %collective-permute-start.3 = (f32[867]{0:T(1024)S(1)}, f32[867]{0:T(1024)S(1)}, u32[]{:S(2)}, u32[]{:S(2)}) collective-permute-start(f32[867]{0:T(1024)S(1)} %get-tuple-element.30), channel_id=1, source_target_pairs={{0,1},{1,0},{2,3},{3,2},{4,5},{5,4},{6,7},{7,6},{8,9},{9,8},{10,11... | collective-permute-start | bytes 10412 | tf_op jit(solution)/shard_map/ppermute | solution.py:397
  28.5 8.0 %collective-permute-start.1 = (f32[64,384]{1,0:T(8,128)S(1)}, f32[64,384]{1,0:T(8,128)S(1)}, u32[]{:S(2)}, u32[]{:S(2)}) collective-permute-start(f32[64,384]{1,0:T(8,128)S(1)} %bitcast.31), channel_id=1, source_target_pairs={{0,2},{1,3},{2,0},{3,1},{4,6},{5,7},{6,4},{7,5},{8,10},{9,11},{10,... | collective-permute-start | bytes 294920 | tf_op jit(solution)/shard_map/ppermute | solution.py:397
  28.9 7.6 %collective-permute-start = (f32[64,384]{1,0:T(8,128)S(1)}, f32[64,384]{1,0:T(8,128)S(1)}, u32[]{:S(2)}, u32[]{:S(2)}) collective-permute-start(f32[64,384]{1,0:T(8,128)S(1)} %bitcast.32), channel_id=1, source_target_pairs={{0,1},{1,0},{2,3},{3,2},{4,5},{5,4},{6,7},{7,6},{8,9},{9,8},{10,11... | collective-permute-start | bytes 294920 | tf_op jit(solution)/shard_map/ppermute | solution.py:397
  31.3 5.4 %collective-permute-start.2 = (f32[64,384]{1,0:T(8,128)S(1)}, f32[64,384]{1,0:T(8,128)S(1)}, u32[]{:S(2)}, u32[]{:S(2)}) collective-permute-start(f32[64,384]{1,0:T(8,128)S(1)} %bitcast.33), channel_id=1, source_target_pairs={{0,3},{1,2},{2,1},{3,0},{4,7},{5,6},{6,5},{7,4},{8,11},{9,10},{10,... | collective-permute-start | bytes 294920 | tf_op jit(solution)/shard_map/ppermute | solution.py:397
  46.2 10.5 %collective-permute-start.7 = (bf16[256,768]{1,0:T(8,128)(2,1)S(1)}, bf16[256,768]{1,0:T(8,128)(2,1)S(1)}, u32[]{:S(2)}, u32[]{:S(2)}) collective-permute-start(bf16[256,768]{1,0:T(8,128)(2,1)S(1)} %get-tuple-element.23), channel_id=1, source_target_pairs={{0,2},{1,3},{2,0},{3,1},{4,6},{5,7},{6,4},{7,5},{8,10},{9,11},{10,... | collective-permute-start | bytes 1179656 | tf_op jit(solution)/shard_map/ppermute | solution.py:397
  46.5 10.1 %collective-permute-start.6 = (bf16[256,768]{1,0:T(8,128)(2,1)S(1)}, bf16[256,768]{1,0:T(8,128)(2,1)S(1)}, u32[]{:S(2)}, u32[]{:S(2)}) collective-permute-start(bf16[256,768]{1,0:T(8,128)(2,1)S(1)} %get-tuple-element.23), channel_id=1, source_target_pairs={{0,1},{1,0},{2,3},{3,2},{4,5},{5,4},{6,7},{7,6},{8,9},{9,8},{10,11... | collective-permute-start | bytes 1179656 | tf_op jit(solution)/shard_map/ppermute | solution.py:397
  56.7 10.1 %collective-permute-start.8 = (bf16[256,768]{1,0:T(8,128)(2,1)S(1)}, bf16[256,768]{1,0:T(8,128)(2,1)S(1)}, u32[]{:S(2)}, u32[]{:S(2)}) collective-permute-start(bf16[256,768]{1,0:T(8,128)(2,1)S(1)} %collective-permute-done.7), channel_id=1, source_target_pairs={{0,1},{1,0},{2,3},{3,2},{4,5},{5,4},{6,7},{7,6},{8,9},{9,8},{10,11... | collective-permute-start | bytes 1179656 | tf_op jit(solution)/shard_map/ppermute | solution.py:397
  57.8 22.0 %all-to-all-start.1 = ((f32[256,1,128]{2,1,0:T(1,128)}), f32[256,1,128]{2,1,0:T(1,128)S(1)}, u32[]{:S(2)}, u32[]{:S(2)}) async-start(f32[256,1,128]{2,1,0:T(1,128)} %bitcast.5), calls=%async_computation.1 | async-start | bytes 262144 | tf_op jit(solution)/shard_map/all_to_all | solution.py:428

commit v5 on v4

--- a/solution.py
+++ b/solution.py
@@ -63,28 +63,24 @@
                 works.remove(work)
 
 
-def demigrate_kernel(first_slab, total, points_ref, nodes_ref, recv_ref, offsets_ref, *refs):
+def demigrate_kernel(first_slab, total, points_ref, nodes_ref, recv, offsets_ref, *refs):
     previous, refs = (refs[:3], refs[3:]) if first_slab else ((), refs)
     last_call = first_slab + points_ref.shape[0] == total
     (gains, index, synth), refs = refs[:3], refs[3:]
     if last_call:
         trace_ref, refs = refs[0], refs[1:]
-    field, recv, near0, near1, *push = refs
+    field, near0, near1, *push = refs
     slabs, owners = points_ref.shape[:2]
     owned = points_ref.shape[2] // 4
     rows = owned // 2
     steps = rows // ROWS
     row_base = first_slab * rows
-    receivers = recv_ref.shape[1]
+    receivers = recv.shape[1]
     part = PIECE
     pieces = BAND // part
     near = (near0, near1)
 
-    for k in range(3):
-        recv[k] = jnp.broadcast_to(recv_ref[k], (receivers, LANES))
-    if previous:
-        synth[...] = previous[2][...]
-    else:
+    if not previous:
         synth[...] = jnp.zeros_like(synth)
     for slab in range(slabs):
         turned = points_ref[slab].T
@@ -150,20 +146,14 @@
             pair // 2, pair % 2, transpose=True,
         )
         wide = [
-            [jnp.broadcast_to(near[slot][k, i : i + 1, :], (8, LANES)) for i in group]
+            [jnp.broadcast_to(near[slot][k, i : i + 1, :], (16, LANES)).astype(BF) for i in group]
             for k in range(4)
         ]
         for tile in range(0, HALF, 16):
-            sample = lax.broadcasted_iota(jnp.int32, (8, LANES), 0).astype(F32)
+            sample = (lax.broadcasted_iota(jnp.int32, (16, LANES), 0) + tile).astype(F32).astype(BF)
             for half in range(2):
                 hat = [
-                    jnp.concatenate(
-                        [
-                            jnp.where(sample + float(tile + up) == wide[half][k], wide[2 + half][k], 0.0)
-                            for up in (0, 8)
-                        ],
-                        axis=0,
-                    ).astype(BF)
+                    jnp.where(sample == wide[half][k], wide[2 + half][k], jnp.zeros((), BF))
                     for k in range(2)
                 ]
                 pltpu.matmul_acc_lhs(
@@ -348,7 +338,6 @@
         outs,
         [
             pltpu.VMEM((4, slabs * rows, LANES), F32),
-            pltpu.VMEM((3, receivers, LANES), F32),
             *[pltpu.VMEM((7, ROWS, LANES), F32) for _ in range(2)],
             *[pltpu.VMEM((2, receivers, LANES), BF) for _ in range(ROWS // 2)],
         ],
@@ -418,7 +407,7 @@
     mine = lax.all_to_all(local, "shot", 0, 0)[:, 0]
     others = jnp.stack([swap(mine, b) for b in range(1, slabs)])
 
-    recv = recv[:, :, None]
+    recv = jnp.broadcast_to(recv[:, :, None], (3, receivers, LANES))
     kept = demigrate_slabs(0, slabs, mine[None], nodes[:1], recv, offsets, [])
     *kept, trace = demigrate_slabs(1, slabs, others, nodes[1:], recv, offsets, kept)
     image = migrate_slabs(slabs, owners, *kept, offsets)

time: 80.6 us -> 79.7 us (0.989)
  transfers between devices with their start and end apart: 11 -> 11, of which waited for: 4 -> 4; matrix products, arithmetic and copies ran while one was open for 12% -> 12% of each run, Pallas kernels for 16% -> 17%
where the time goes in v5:
time: 79.7 us; the launch traced here: 79.4 us
  starting transfers between devices  32.6 us (41%)
  Pallas kernels  23.3 us (29%)
  waiting for transfers between devices  12.6 us (16%)
  local copies, waits for them, and re-layouts  6.04 us (8%)
  other arithmetic  4.03 us (5%)
  between operations  0.86 us (1%)
    pallas_call x3, Pallas kernels, call(): pl.pallas_call(kernel, out_shape=outs, in_specs=[pl.BlockSpec(memory_spac...  21.8 us
    all_to_all x1, starting transfers between devices, body(): mine = lax.all_to_all(local, 'shot', 0, 0)[:, 0]  15.1 us
    all_to_all x1, waiting for transfers between devices, body(): spread = lax.all_to_all(image, ('shot', 'slab'), 0, 0)  10.2 us
    all_to_all x1, starting transfers between devices, body(): spread = lax.all_to_all(image, ('shot', 'slab'), 0, 0)  8.83 us
    ppermute x9, starting transfers between devices, swap(): return array if b == 0 else lax.ppermute(array, 'slab', swaps[b])  8.62 us
    pad x1, other arithmetic, body(): jnp.pad(jnp.stack([first, second, third, fourth]).astype(F32), ((0, 0), (...  2.58 us
    concatenate x1, local copies, waits for them, and re-layouts, body(): jnp.concatenate([jnp.stack([pick(band_offsets, b) for b in range(slabs)])...  2.51 us
    dynamic_slice x3, local copies, waits for them, and re-layouts, pick(): return lax.dynamic_index_in_dim(array, me ^ b, axis, keepdims=False)  2.39 us
  transfers between devices with their start and end apart: 11, of which 4 were waited for; matrix products, arithmetic and copies ran while one was open for 12% of the time, Pallas kernels for 17%

profile of v5, /device:TPU:1, one launch (start us, length us, event | category | flops | bytes accessed | tf_op | source)
XLA Modules:
  0.0 79.4 jit_solution(16755423290879078899)
XLA Ops:
  0.6 1.5 %shard_map.95 = f32[64,1,384]{2,1,0:T(1,128)} custom-call(f32[1,96]{1,0:T(1,128)} %amplitudes_ref.1, s32[1,96]{1,0:T(1,128)} %depth_ref.1, s32[2,1,96]{2,1,0:T(1,128)} %lateral_ref.1, f32[3,1,96]{2,1,0:T(1,128)} %jitter_ref.1), custom_call_target="tpu_custom_call" | custom-call | tf_op jit(solution)/shard_map/pallas_call | solution.py:379
  2.1 15.1 %all-to-all-start = ((f32[64,1,384]{2,1,0:T(1,128)}), f32[64,1,384]{2,1,0:T(1,128)S(1)}, u32[]{:S(2)}, u32[]{:S(2)}) async-start(f32[64,1,384]{2,1,0:T(1,128)} %shard_map.95), calls=%async_computation | async-start | bytes 196608 | tf_op jit(solution)/shard_map/all_to_all | solution.py:407
  17.3 0.8 dynamic-slice_reduce_fusion
  18.0 1.2 %collective-permute-start.5 = (f32[867]{0:T(1024)S(1)}, f32[867]{0:T(1024)S(1)}, u32[]{:S(2)}, u32[]{:S(2)}) collective-permute-start(f32[867]{0:T(1024)S(1)} %get-tuple-element.28), channel_id=1, source_target_pairs={{0,3},{1,2},{2,1},{3,0},{4,7},{5,6},{6,5},{7,4},{8,11},{9,10},{10,... | collective-permute-start | bytes 10412 | tf_op jit(solution)/shard_map/ppermute | solution.py:386
  19.3 1.2 %collective-permute-start.4 = (f32[867]{0:T(1024)S(1)}, f32[867]{0:T(1024)S(1)}, u32[]{:S(2)}, u32[]{:S(2)}) collective-permute-start(f32[867]{0:T(1024)S(1)} %get-tuple-element.29), channel_id=1, source_target_pairs={{0,2},{1,3},{2,0},{3,1},{4,6},{5,7},{6,4},{7,5},{8,10},{9,11},{10,... | collective-permute-start | bytes 10412 | tf_op jit(solution)/shard_map/ppermute | solution.py:386
  20.4 0.7 convert_multiply_fusion
  21.1 0.1 stack.56
  21.3 0.2 fusion.8
  21.5 1.4 %fusion.10 = (s32[1]{0:T(128)}, s32[1]{0:T(128)}, s32[1]{0:T(128)}, s32[1]{0:T(128)}) fusion(s32[4]{0:T(128)} %param.15, s32[]{:T(128)S(6)} %select_n.68, s32[]{:T(128)S(6)} %select_n.66, s32[]{:T(128)S(6)} %select_n.65, s32[]{:T(128)S(6)} %select_n.67), kind=kLoop, calls=%fused_computation.40 | loop fusion | bytes 48 | tf_op jit(solution)/shard_map/jit(dynamic_index_in_dim)/dynamic_slice | solution.py:389
  22.9 2.5 %concatenate.8.offsets_ref = s32[10]{0:T(128)S(1)} concatenate(s32[1]{0:T(128)} %get-tuple-element.47, s32[1]{0:T(128)} %get-tuple-element.46, s32[1]{0:T(128)} %get-tuple-element.48, s32[1]{0:T(128)} %get-tuple-element.45, s32[2]{0:T(128)S(1)} %fusion.8, s32[4]{0:T(128)S(1)} %iota_xor_fusion), dimensions={0} | concatenate | bytes 80 | tf_op jit(solution)/shard_map/concatenate | solution.py:401
  25.4 0.1 stack.57
  25.6 0.1 stack.58
  25.7 0.1 stack.59
  25.8 0.1 fusion.9
  26.4 2.1 %all-to-all-done = f32[64,1,384]{2,1,0:T(1,128)S(1)} async-done(((f32[64,1,384]{2,1,0:T(1,128)}), f32[64,1,384]{2,1,0:T(1,128)S(1)}, u32[]{:S(2)}, u32[]{:S(2)}) %all-to-all-start) | async-done | bytes 98336 | tf_op jit(solution)/shard_map/all_to_all | solution.py:407
  28.5 0.4 collective-permute-start.1
  28.9 2.4 %collective-permute-start = (f32[64,384]{1,0:T(8,128)S(1)}, f32[64,384]{1,0:T(8,128)S(1)}, u32[]{:S(2)}, u32[]{:S(2)}) collective-permute-start(f32[64,384]{1,0:T(8,128)S(1)} %bitcast.30), channel_id=1, source_target_pairs={{0,1},{1,0},{2,3},{3,2},{4,5},{5,4},{6,7},{7,6},{8,9},{9,8},{10,11... | collective-permute-start | bytes 294920 | tf_op jit(solution)/shard_map/ppermute | solution.py:386
  31.3 1.0 %collective-permute-start.2 = (f32[64,384]{1,0:T(8,128)S(1)}, f32[64,384]{1,0:T(8,128)S(1)}, u32[]{:S(2)}, u32[]{:S(2)}) collective-permute-start(f32[64,384]{1,0:T(8,128)S(1)} %bitcast.31), channel_id=1, source_target_pairs={{0,3},{1,2},{2,1},{3,0},{4,7},{5,6},{6,5},{7,4},{8,11},{9,10},{10,... | collective-permute-start | bytes 294920 | tf_op jit(solution)/shard_map/ppermute | solution.py:386
  32.3 0.2 broadcast_in_dim.4.recv
  32.5 4.1 %shard_map.96 = (bf16[192,256,128]{2,1,0:T(8,128)(2,1)S(1)}, f32[4,192,128]{2,1,0:T(8,128)S(1)}, f32[2,1024,128]{2,1,0:T(8,128)S(1)}) custom-call(f32[1,64,384]{2,1,0:T(8,128)S(1)} %bitcast.32, f32[1,24,128]{2,1,0:T(8,128)S(1)} %pad_maximum_fusion.2.nodes_ref, f32[3,256,128]{2,1,0:T(8,128)S(1)} %broadcast_in_dim.4.recv, s32[10]{0:T(128)S(1)} %concatenate.8.offsets_ref), custom_call_target="tpu_custom_call" | custom-call | tf_op jit(solution)/shard_map/pallas_call | solution.py:314
  36.6 0.1 collective-permute-done.2
  36.7 8.7 %shard_map.97 = (bf16[192,256,128]{2,1,0:T(8,128)(2,1)S(1)}, f32[4,192,128]{2,1,0:T(8,128)S(1)}, f32[2,1024,128]{2,1,0:T(8,128)S(1)}, bf16[256,768]{1,0:T(8,128)(2,1)S(1)}) custom-call(f32[3,64,384]{2,1,0:T(8,128)S(1)} %pad_maximum_fusion.points_ref, f32[3,24,128]{2,1,0:T(8,128)S(1)} %slice.44.nodes_ref, ...), custom_call_target="tpu_custom_call", output_to_operand_aliasing={{0}: (4, {}), {1}: (5, {}), {2}: (6, {})} | custom-call | tf_op jit(solution)/shard_map/pallas_call | solution.py:314
  45.4 0.4 collective-permute-start.7
  45.9 0.7 collective-permute-start.6
  46.6 9.0 %shard_map.98 = f32[256,128]{1,0:T(8,128)} custom-call(bf16[192,256,128]{2,1,0:T(8,128)(2,1)S(1)} %get-tuple-element.20.gains, f32[4,192,128]{2,1,0:T(8,128)S(1)} %get-tuple-element.21.index, f32[2,1024,128]{2,1,0:T(8,128)S(1)} %get-tuple-element.22.synth, s32[10]{0:T(128)S(1)} %concatenate.8.offsets_ref), custom_call_target="tpu_custom_call" | custom-call | tf_op jit(solution)/shard_map/pallas_call | solution.py:314
  55.6 0.2 collective-permute-done.7
  55.8 1.3 %collective-permute-start.8 = (bf16[256,768]{1,0:T(8,128)(2,1)S(1)}, bf16[256,768]{1,0:T(8,128)(2,1)S(1)}, u32[]{:S(2)}, u32[]{:S(2)}) collective-permute-start(bf16[256,768]{1,0:T(8,128)(2,1)S(1)} %collective-permute-done.7), channel_id=1, source_target_pairs={{0,1},{1,0},{2,3},{3,2},{4,5},{5,4},{6,7},{7,6},{8,9},{9,8},{10,11... | collective-permute-start | bytes 1179656 | tf_op jit(solution)/shard_map/ppermute | solution.py:386
  57.1 8.8 %all-to-all-start.1 = ((f32[256,1,128]{2,1,0:T(1,128)}), f32[256,1,128]{2,1,0:T(1,128)S(1)}, u32[]{:S(2)}, u32[]{:S(2)}) async-start(f32[256,1,128]{2,1,0:T(1,128)} %bitcast.4), calls=%async_computation.1 | async-start | bytes 262144 | tf_op jit(solution)/shard_map/all_to_all | solution.py:417
  65.9 0.1 select_bitcast_fusion.3
  66.1 2.6 %fusion.7 = f32[4,256,1024]{2,1,0:T(8,128)} fusion(bf16[1,256,768]{2,1,0:T(8,128)(2,1)S(1)} %get-tuple-element.35, bf16[1,256,768]{2,1,0:T(8,128)(2,1)S(1)} %get-tuple-element.34, bf16[1,256,768]{2,1,0:T(8,128)(2,1)S(1)} %get-tuple-element.33, bf16[1,256,768]{2,1,0:T(8,128)(2,1)S(1)} %get-tuple-element.32), kind=kLoop, calls=%fused_computation.8 | loop fusion | flops 13631488 | bytes 5767168 | tf_op jit(solution)/shard_map/jit(_pad)/pad | solution.py:429
  68.6 10.2 %all-to-all-done.1 = f32[256,1,128]{2,1,0:T(1,128)S(1)} async-done(((f32[256,1,128]{2,1,0:T(1,128)}), f32[256,1,128]{2,1,0:T(1,128)S(1)}, u32[]{:S(2)}, u32[]{:S(2)}) %all-to-all-start.1) | async-done | bytes 131104 | tf_op jit(solution)/shard_map/all_to_all | solution.py:417
  78.9 0.6 slice_reduce_fusion
  (26 shorter events, 0.5 us)
Async XLA Ops:
  0.6 20.7 %copy-start = (s32[2,4]{1,0:T(2,128)S(1)}, s32[2,4]{1,0:T(2,128)}, u32[]{:S(2)}) copy-start(s32[2,4]{1,0:T(2,128)} %param.13) | copy-start | bytes 100
  2.1 26.3 %all-to-all-start = ((f32[64,1,384]{2,1,0:T(1,128)}), f32[64,1,384]{2,1,0:T(1,128)S(1)}, u32[]{:S(2)}, u32[]{:S(2)}) async-start(f32[64,1,384]{2,1,0:T(1,128)} %shard_map.95), calls=%async_computation | async-start | bytes 196608 | tf_op jit(solution)/shard_map/all_to_all | solution.py:407
  18.0 7.7 %collective-permute-start.5 = (f32[867]{0:T(1024)S(1)}, f32[867]{0:T(1024)S(1)}, u32[]{:S(2)}, u32[]{:S(2)}) collective-permute-start(f32[867]{0:T(1024)S(1)} %get-tuple-element.28), channel_id=1, source_target_pairs={{0,3},{1,2},{2,1},{3,0},{4,7},{5,6},{6,5},{7,4},{8,11},{9,10},{10,... | collective-permute-start | bytes 10412 | tf_op jit(solution)/shard_map/ppermute | solution.py:386
  19.3 6.3 %collective-permute-start.4 = (f32[867]{0:T(1024)S(1)}, f32[867]{0:T(1024)S(1)}, u32[]{:S(2)}, u32[]{:S(2)}) collective-permute-start(f32[867]{0:T(1024)S(1)} %get-tuple-element.29), channel_id=1, source_target_pairs={{0,2},{1,3},{2,0},{3,1},{4,6},{5,7},{6,4},{7,5},{8,10},{9,11},{10,... | collective-permute-start | bytes 10412 | tf_op jit(solution)/shard_map/ppermute | solution.py:386
  20.4 5.0 %collective-permute-start.3 = (f32[867]{0:T(1024)S(1)}, f32[867]{0:T(1024)S(1)}, u32[]{:S(2)}, u32[]{:S(2)}) collective-permute-start(f32[867]{0:T(1024)S(1)} %get-tuple-element.30), channel_id=1, source_target_pairs={{0,1},{1,0},{2,3},{3,2},{4,5},{5,4},{6,7},{7,6},{8,9},{9,8},{10,11... | collective-permute-start | bytes 10412 | tf_op jit(solution)/shard_map/ppermute | solution.py:386
  28.5 8.1 %collective-permute-start.1 = (f32[64,384]{1,0:T(8,128)S(1)}, f32[64,384]{1,0:T(8,128)S(1)}, u32[]{:S(2)}, u32[]{:S(2)}) collective-permute-start(f32[64,384]{1,0:T(8,128)S(1)} %bitcast.29), channel_id=1, source_target_pairs={{0,2},{1,3},{2,0},{3,1},{4,6},{5,7},{6,4},{7,5},{8,10},{9,11},{10,... | collective-permute-start | bytes 294920 | tf_op jit(solution)/shard_map/ppermute | solution.py:386
  28.9 7.7 %collective-permute-start = (f32[64,384]{1,0:T(8,128)S(1)}, f32[64,384]{1,0:T(8,128)S(1)}, u32[]{:S(2)}, u32[]{:S(2)}) collective-permute-start(f32[64,384]{1,0:T(8,128)S(1)} %bitcast.30), channel_id=1, source_target_pairs={{0,1},{1,0},{2,3},{3,2},{4,5},{5,4},{6,7},{7,6},{8,9},{9,8},{10,11... | collective-permute-start | bytes 294920 | tf_op jit(solution)/shard_map/ppermute | solution.py:386
  31.3 5.4 %collective-permute-start.2 = (f32[64,384]{1,0:T(8,128)S(1)}, f32[64,384]{1,0:T(8,128)S(1)}, u32[]{:S(2)}, u32[]{:S(2)}) collective-permute-start(f32[64,384]{1,0:T(8,128)S(1)} %bitcast.31), channel_id=1, source_target_pairs={{0,3},{1,2},{2,1},{3,0},{4,7},{5,6},{6,5},{7,4},{8,11},{9,10},{10,... | collective-permute-start | bytes 294920 | tf_op jit(solution)/shard_map/ppermute | solution.py:386
  45.4 10.3 %collective-permute-start.7 = (bf16[256,768]{1,0:T(8,128)(2,1)S(1)}, bf16[256,768]{1,0:T(8,128)(2,1)S(1)}, u32[]{:S(2)}, u32[]{:S(2)}) collective-permute-start(bf16[256,768]{1,0:T(8,128)(2,1)S(1)} %get-tuple-element.23), channel_id=1, source_target_pairs={{0,2},{1,3},{2,0},{3,1},{4,6},{5,7},{6,4},{7,5},{8,10},{9,11},{10,... | collective-permute-start | bytes 1179656 | tf_op jit(solution)/shard_map/ppermute | solution.py:386
  45.9 9.9 %collective-permute-start.6 = (bf16[256,768]{1,0:T(8,128)(2,1)S(1)}, bf16[256,768]{1,0:T(8,128)(2,1)S(1)}, u32[]{:S(2)}, u32[]{:S(2)}) collective-permute-start(bf16[256,768]{1,0:T(8,128)(2,1)S(1)} %get-tuple-element.23), channel_id=1, source_target_pairs={{0,1},{1,0},{2,3},{3,2},{4,5},{5,4},{6,7},{7,6},{8,9},{9,8},{10,11... | collective-permute-start | bytes 1179656 | tf_op jit(solution)/shard_map/ppermute | solution.py:386
  55.8 10.1 %collective-permute-start.8 = (bf16[256,768]{1,0:T(8,128)(2,1)S(1)}, bf16[256,768]{1,0:T(8,128)(2,1)S(1)}, u32[]{:S(2)}, u32[]{:S(2)}) collective-permute-start(bf16[256,768]{1,0:T(8,128)(2,1)S(1)} %collective-permute-done.7), channel_id=1, source_target_pairs={{0,1},{1,0},{2,3},{3,2},{4,5},{5,4},{6,7},{7,6},{8,9},{9,8},{10,11... | collective-permute-start | bytes 1179656 | tf_op jit(solution)/shard_map/ppermute | solution.py:386
  57.1 21.8 %all-to-all-start.1 = ((f32[256,1,128]{2,1,0:T(1,128)}), f32[256,1,128]{2,1,0:T(1,128)S(1)}, u32[]{:S(2)}, u32[]{:S(2)}) async-start(f32[256,1,128]{2,1,0:T(1,128)} %bitcast.4), calls=%async_computation.1 | async-start | bytes 262144 | tf_op jit(solution)/shard_map/all_to_all | solution.py:417

commit v6 on v5

--- a/solution.py
+++ b/solution.py
@@ -19,7 +19,7 @@
 ROWS = 8
 MXU = 256
 PIECE = 16
-MIG_SPAN = 6
+MIG_SPAN = 12
 VMEM_LIMIT = 8 * 1024 * 1024
 BF = jnp.bfloat16
 F32 = jnp.float32

time: 79.7 us -> 79.7 us (level)
  transfers between devices with their start and end apart: 11 -> 11, of which waited for: 4 -> 4; matrix products, arithmetic and copies ran while one was open for 12% -> 12% of each run, Pallas kernels for 17% -> 16%
where the time goes in v6:
time: 79.7 us; the launch traced here: 79.4 us
  starting transfers between devices  32.6 us (41%)
  Pallas kernels  23 us (29%)
  waiting for transfers between devices  13 us (16%)
  local copies, waits for them, and re-layouts  6.04 us (8%)
  other arithmetic  4.03 us (5%)
  between operations  0.86 us (1%)
    pallas_call x3, Pallas kernels, call(): pl.pallas_call(kernel, out_shape=outs, in_specs=[pl.BlockSpec(memory_spac...  21.5 us
    all_to_all x1, starting transfers between devices, body(): mine = lax.all_to_all(local, 'shot', 0, 0)[:, 0]  15.1 us
    all_to_all x1, waiting for transfers between devices, body(): spread = lax.all_to_all(image, ('shot', 'slab'), 0, 0)  10.2 us
    all_to_all x1, starting transfers between devices, body(): spread = lax.all_to_all(image, ('shot', 'slab'), 0, 0)  8.83 us
    ppermute x9, starting transfers between devices, swap(): return array if b == 0 else lax.ppermute(array, 'slab', swaps[b])  8.62 us
    pad x1, other arithmetic, body(): jnp.pad(jnp.stack([first, second, third, fourth]).astype(F32), ((0, 0), (...  2.58 us
    concatenate x1, local copies, waits for them, and re-layouts, body(): jnp.concatenate([jnp.stack([pick(band_offsets, b) for b in range(slabs)])...  2.51 us
    dynamic_slice x3, local copies, waits for them, and re-layouts, pick(): return lax.dynamic_index_in_dim(array, me ^ b, axis, keepdims=False)  2.39 us
  transfers between devices with their start and end apart: 11, of which 4 were waited for; matrix products, arithmetic and copies ran while one was open for 12% of the time, Pallas kernels for 16%

profile of v6, /device:TPU:1, one launch (start us, length us, event | category | flops | bytes accessed | tf_op | source)
XLA Modules:
  0.0 79.4 jit_solution(2014402990090821503)
XLA Ops:
  0.6 1.5 %shard_map.95 = f32[64,1,384]{2,1,0:T(1,128)} custom-call(f32[1,96]{1,0:T(1,128)} %amplitudes_ref.1, s32[1,96]{1,0:T(1,128)} %depth_ref.1, s32[2,1,96]{2,1,0:T(1,128)} %lateral_ref.1, f32[3,1,96]{2,1,0:T(1,128)} %jitter_ref.1), custom_call_target="tpu_custom_call" | custom-call | tf_op jit(solution)/shard_map/pallas_call | solution.py:379
  2.1 15.1 %all-to-all-start = ((f32[64,1,384]{2,1,0:T(1,128)}), f32[64,1,384]{2,1,0:T(1,128)S(1)}, u32[]{:S(2)}, u32[]{:S(2)}) async-start(f32[64,1,384]{2,1,0:T(1,128)} %shard_map.95), calls=%async_computation | async-start | bytes 196608 | tf_op jit(solution)/shard_map/all_to_all | solution.py:407
  17.3 0.8 dynamic-slice_reduce_fusion
  18.0 1.2 %collective-permute-start.5 = (f32[867]{0:T(1024)S(1)}, f32[867]{0:T(1024)S(1)}, u32[]{:S(2)}, u32[]{:S(2)}) collective-permute-start(f32[867]{0:T(1024)S(1)} %get-tuple-element.28), channel_id=1, source_target_pairs={{0,3},{1,2},{2,1},{3,0},{4,7},{5,6},{6,5},{7,4},{8,11},{9,10},{10,... | collective-permute-start | bytes 10412 | tf_op jit(solution)/shard_map/ppermute | solution.py:386
  19.3 1.2 %collective-permute-start.4 = (f32[867]{0:T(1024)S(1)}, f32[867]{0:T(1024)S(1)}, u32[]{:S(2)}, u32[]{:S(2)}) collective-permute-start(f32[867]{0:T(1024)S(1)} %get-tuple-element.29), channel_id=1, source_target_pairs={{0,2},{1,3},{2,0},{3,1},{4,6},{5,7},{6,4},{7,5},{8,10},{9,11},{10,... | collective-permute-start | bytes 10412 | tf_op jit(solution)/shard_map/ppermute | solution.py:386
  20.4 0.7 convert_multiply_fusion
  21.1 0.1 stack.56
  21.3 0.2 fusion.8
  21.5 1.4 %fusion.10 = (s32[1]{0:T(128)}, s32[1]{0:T(128)}, s32[1]{0:T(128)}, s32[1]{0:T(128)}) fusion(s32[4]{0:T(128)} %param.15, s32[]{:T(128)S(6)} %select_n.68, s32[]{:T(128)S(6)} %select_n.66, s32[]{:T(128)S(6)} %select_n.65, s32[]{:T(128)S(6)} %select_n.67), kind=kLoop, calls=%fused_computation.40 | loop fusion | bytes 48 | tf_op jit(solution)/shard_map/jit(dynamic_index_in_dim)/dynamic_slice | solution.py:389
  22.9 2.5 %concatenate.8.offsets_ref = s32[10]{0:T(128)S(1)} concatenate(s32[1]{0:T(128)} %get-tuple-element.47, s32[1]{0:T(128)} %get-tuple-element.46, s32[1]{0:T(128)} %get-tuple-element.48, s32[1]{0:T(128)} %get-tuple-element.45, s32[2]{0:T(128)S(1)} %fusion.8, s32[4]{0:T(128)S(1)} %iota_xor_fusion), dimensions={0} | concatenate | bytes 80 | tf_op jit(solution)/shard_map/concatenate | solution.py:401
  25.4 0.1 stack.57
  25.6 0.1 stack.58
  25.7 0.1 stack.59
  25.8 0.1 fusion.9
  26.4 2.1 %all-to-all-done = f32[64,1,384]{2,1,0:T(1,128)S(1)} async-done(((f32[64,1,384]{2,1,0:T(1,128)}), f32[64,1,384]{2,1,0:T(1,128)S(1)}, u32[]{:S(2)}, u32[]{:S(2)}) %all-to-all-start) | async-done | bytes 98336 | tf_op jit(solution)/shard_map/all_to_all | solution.py:407
  28.5 0.4 collective-permute-start.1
  28.9 2.4 %collective-permute-start = (f32[64,384]{1,0:T(8,128)S(1)}, f32[64,384]{1,0:T(8,128)S(1)}, u32[]{:S(2)}, u32[]{:S(2)}) collective-permute-start(f32[64,384]{1,0:T(8,128)S(1)} %bitcast.30), channel_id=1, source_target_pairs={{0,1},{1,0},{2,3},{3,2},{4,5},{5,4},{6,7},{7,6},{8,9},{9,8},{10,11... | collective-permute-start | bytes 294920 | tf_op jit(solution)/shard_map/ppermute | solution.py:386
  31.3 1.0 %collective-permute-start.2 = (f32[64,384]{1,0:T(8,128)S(1)}, f32[64,384]{1,0:T(8,128)S(1)}, u32[]{:S(2)}, u32[]{:S(2)}) collective-permute-start(f32[64,384]{1,0:T(8,128)S(1)} %bitcast.31), channel_id=1, source_target_pairs={{0,3},{1,2},{2,1},{3,0},{4,7},{5,6},{6,5},{7,4},{8,11},{9,10},{10,... | collective-permute-start | bytes 294920 | tf_op jit(solution)/shard_map/ppermute | solution.py:386
  32.3 0.2 broadcast_in_dim.4.recv
  32.5 4.1 %shard_map.96 = (bf16[192,256,128]{2,1,0:T(8,128)(2,1)S(1)}, f32[4,192,128]{2,1,0:T(8,128)S(1)}, f32[2,1024,128]{2,1,0:T(8,128)S(1)}) custom-call(f32[1,64,384]{2,1,0:T(8,128)S(1)} %bitcast.32, f32[1,24,128]{2,1,0:T(8,128)S(1)} %pad_maximum_fusion.2.nodes_ref, f32[3,256,128]{2,1,0:T(8,128)S(1)} %broadcast_in_dim.4.recv, s32[10]{0:T(128)S(1)} %concatenate.8.offsets_ref), custom_call_target="tpu_custom_call" | custom-call | tf_op jit(solution)/shard_map/pallas_call | solution.py:314
  36.6 0.1 collective-permute-done.2
  36.7 8.7 %shard_map.97 = (bf16[192,256,128]{2,1,0:T(8,128)(2,1)S(1)}, f32[4,192,128]{2,1,0:T(8,128)S(1)}, f32[2,1024,128]{2,1,0:T(8,128)S(1)}, bf16[256,768]{1,0:T(8,128)(2,1)S(1)}) custom-call(f32[3,64,384]{2,1,0:T(8,128)S(1)} %pad_maximum_fusion.points_ref, f32[3,24,128]{2,1,0:T(8,128)S(1)} %slice.44.nodes_ref, ...), custom_call_target="tpu_custom_call", output_to_operand_aliasing={{0}: (4, {}), {1}: (5, {}), {2}: (6, {})} | custom-call | tf_op jit(solution)/shard_map/pallas_call | solution.py:314
  45.4 0.4 collective-permute-start.7
  45.9 0.7 collective-permute-start.6
  46.6 8.7 %shard_map.98 = f32[256,128]{1,0:T(8,128)} custom-call(bf16[192,256,128]{2,1,0:T(8,128)(2,1)S(1)} %get-tuple-element.20.gains, f32[4,192,128]{2,1,0:T(8,128)S(1)} %get-tuple-element.21.index, f32[2,1024,128]{2,1,0:T(8,128)S(1)} %get-tuple-element.22.synth, s32[10]{0:T(128)S(1)} %concatenate.8.offsets_ref), custom_call_target="tpu_custom_call" | custom-call | tf_op jit(solution)/shard_map/pallas_call | solution.py:314
  55.2 0.5 collective-permute-done.7
  55.8 1.3 %collective-permute-start.8 = (bf16[256,768]{1,0:T(8,128)(2,1)S(1)}, bf16[256,768]{1,0:T(8,128)(2,1)S(1)}, u32[]{:S(2)}, u32[]{:S(2)}) collective-permute-start(bf16[256,768]{1,0:T(8,128)(2,1)S(1)} %collective-permute-done.7), channel_id=1, source_target_pairs={{0,1},{1,0},{2,3},{3,2},{4,5},{5,4},{6,7},{7,6},{8,9},{9,8},{10,11... | collective-permute-start | bytes 1179656 | tf_op jit(solution)/shard_map/ppermute | solution.py:386
  57.1 8.8 %all-to-all-start.1 = ((f32[256,1,128]{2,1,0:T(1,128)}), f32[256,1,128]{2,1,0:T(1,128)S(1)}, u32[]{:S(2)}, u32[]{:S(2)}) async-start(f32[256,1,128]{2,1,0:T(1,128)} %bitcast.4), calls=%async_computation.1 | async-start | bytes 262144 | tf_op jit(solution)/shard_map/all_to_all | solution.py:417
  65.9 0.1 select_bitcast_fusion.3
  66.1 2.6 %fusion.7 = f32[4,256,1024]{2,1,0:T(8,128)} fusion(bf16[1,256,768]{2,1,0:T(8,128)(2,1)S(1)} %get-tuple-element.35, bf16[1,256,768]{2,1,0:T(8,128)(2,1)S(1)} %get-tuple-element.34, bf16[1,256,768]{2,1,0:T(8,128)(2,1)S(1)} %get-tuple-element.33, bf16[1,256,768]{2,1,0:T(8,128)(2,1)S(1)} %get-tuple-element.32), kind=kLoop, calls=%fused_computation.8 | loop fusion | flops 13631488 | bytes 5767168 | tf_op jit(solution)/shard_map/jit(_pad)/pad | solution.py:429
  68.6 10.2 %all-to-all-done.1 = f32[256,1,128]{2,1,0:T(1,128)S(1)} async-done(((f32[256,1,128]{2,1,0:T(1,128)}), f32[256,1,128]{2,1,0:T(1,128)S(1)}, u32[]{:S(2)}, u32[]{:S(2)}) %all-to-all-start.1) | async-done | bytes 131104 | tf_op jit(solution)/shard_map/all_to_all | solution.py:417
  78.9 0.6 slice_reduce_fusion
  (26 shorter events, 0.5 us)
Async XLA Ops:
  0.6 20.7 %copy-start = (s32[2,4]{1,0:T(2,128)S(1)}, s32[2,4]{1,0:T(2,128)}, u32[]{:S(2)}) copy-start(s32[2,4]{1,0:T(2,128)} %param.13) | copy-start | bytes 100
  2.1 26.3 %all-to-all-start = ((f32[64,1,384]{2,1,0:T(1,128)}), f32[64,1,384]{2,1,0:T(1,128)S(1)}, u32[]{:S(2)}, u32[]{:S(2)}) async-start(f32[64,1,384]{2,1,0:T(1,128)} %shard_map.95), calls=%async_computation | async-start | bytes 196608 | tf_op jit(solution)/shard_map/all_to_all | solution.py:407
  18.0 7.7 %collective-permute-start.5 = (f32[867]{0:T(1024)S(1)}, f32[867]{0:T(1024)S(1)}, u32[]{:S(2)}, u32[]{:S(2)}) collective-permute-start(f32[867]{0:T(1024)S(1)} %get-tuple-element.28), channel_id=1, source_target_pairs={{0,3},{1,2},{2,1},{3,0},{4,7},{5,6},{6,5},{7,4},{8,11},{9,10},{10,... | collective-permute-start | bytes 10412 | tf_op jit(solution)/shard_map/ppermute | solution.py:386
  19.3 6.3 %collective-permute-start.4 = (f32[867]{0:T(1024)S(1)}, f32[867]{0:T(1024)S(1)}, u32[]{:S(2)}, u32[]{:S(2)}) collective-permute-start(f32[867]{0:T(1024)S(1)} %get-tuple-element.29), channel_id=1, source_target_pairs={{0,2},{1,3},{2,0},{3,1},{4,6},{5,7},{6,4},{7,5},{8,10},{9,11},{10,... | collective-permute-start | bytes 10412 | tf_op jit(solution)/shard_map/ppermute | solution.py:386
  20.4 5.0 %collective-permute-start.3 = (f32[867]{0:T(1024)S(1)}, f32[867]{0:T(1024)S(1)}, u32[]{:S(2)}, u32[]{:S(2)}) collective-permute-start(f32[867]{0:T(1024)S(1)} %get-tuple-element.30), channel_id=1, source_target_pairs={{0,1},{1,0},{2,3},{3,2},{4,5},{5,4},{6,7},{7,6},{8,9},{9,8},{10,11... | collective-permute-start | bytes 10412 | tf_op jit(solution)/shard_map/ppermute | solution.py:386
  28.5 8.1 %collective-permute-start.1 = (f32[64,384]{1,0:T(8,128)S(1)}, f32[64,384]{1,0:T(8,128)S(1)}, u32[]{:S(2)}, u32[]{:S(2)}) collective-permute-start(f32[64,384]{1,0:T(8,128)S(1)} %bitcast.29), channel_id=1, source_target_pairs={{0,2},{1,3},{2,0},{3,1},{4,6},{5,7},{6,4},{7,5},{8,10},{9,11},{10,... | collective-permute-start | bytes 294920 | tf_op jit(solution)/shard_map/ppermute | solution.py:386
  28.9 7.7 %collective-permute-start = (f32[64,384]{1,0:T(8,128)S(1)}, f32[64,384]{1,0:T(8,128)S(1)}, u32[]{:S(2)}, u32[]{:S(2)}) collective-permute-start(f32[64,384]{1,0:T(8,128)S(1)} %bitcast.30), channel_id=1, source_target_pairs={{0,1},{1,0},{2,3},{3,2},{4,5},{5,4},{6,7},{7,6},{8,9},{9,8},{10,11... | collective-permute-start | bytes 294920 | tf_op jit(solution)/shard_map/ppermute | solution.py:386
  31.3 5.4 %collective-permute-start.2 = (f32[64,384]{1,0:T(8,128)S(1)}, f32[64,384]{1,0:T(8,128)S(1)}, u32[]{:S(2)}, u32[]{:S(2)}) collective-permute-start(f32[64,384]{1,0:T(8,128)S(1)} %bitcast.31), channel_id=1, source_target_pairs={{0,3},{1,2},{2,1},{3,0},{4,7},{5,6},{6,5},{7,4},{8,11},{9,10},{10,... | collective-permute-start | bytes 294920 | tf_op jit(solution)/shard_map/ppermute | solution.py:386
  45.4 10.3 %collective-permute-start.7 = (bf16[256,768]{1,0:T(8,128)(2,1)S(1)}, bf16[256,768]{1,0:T(8,128)(2,1)S(1)}, u32[]{:S(2)}, u32[]{:S(2)}) collective-permute-start(bf16[256,768]{1,0:T(8,128)(2,1)S(1)} %get-tuple-element.23), channel_id=1, source_target_pairs={{0,2},{1,3},{2,0},{3,1},{4,6},{5,7},{6,4},{7,5},{8,10},{9,11},{10,... | collective-permute-start | bytes 1179656 | tf_op jit(solution)/shard_map/ppermute | solution.py:386
  45.9 9.9 %collective-permute-start.6 = (bf16[256,768]{1,0:T(8,128)(2,1)S(1)}, bf16[256,768]{1,0:T(8,128)(2,1)S(1)}, u32[]{:S(2)}, u32[]{:S(2)}) collective-permute-start(bf16[256,768]{1,0:T(8,128)(2,1)S(1)} %get-tuple-element.23), channel_id=1, source_target_pairs={{0,1},{1,0},{2,3},{3,2},{4,5},{5,4},{6,7},{7,6},{8,9},{9,8},{10,11... | collective-permute-start | bytes 1179656 | tf_op jit(solution)/shard_map/ppermute | solution.py:386
  55.8 10.1 %collective-permute-start.8 = (bf16[256,768]{1,0:T(8,128)(2,1)S(1)}, bf16[256,768]{1,0:T(8,128)(2,1)S(1)}, u32[]{:S(2)}, u32[]{:S(2)}) collective-permute-start(bf16[256,768]{1,0:T(8,128)(2,1)S(1)} %collective-permute-done.7), channel_id=1, source_target_pairs={{0,1},{1,0},{2,3},{3,2},{4,5},{5,4},{6,7},{7,6},{8,9},{9,8},{10,11... | collective-permute-start | bytes 1179656 | tf_op jit(solution)/shard_map/ppermute | solution.py:386
  57.1 21.8 %all-to-all-start.1 = ((f32[256,1,128]{2,1,0:T(1,128)}), f32[256,1,128]{2,1,0:T(1,128)S(1)}, u32[]{:S(2)}, u32[]{:S(2)}) async-start(f32[256,1,128]{2,1,0:T(1,128)} %bitcast.4), calls=%async_computation.1 | async-start | bytes 262144 | tf_op jit(solution)/shard_map/all_to_all | solution.py:417
